TPU v7x, 256 devices: a whole 4x4x8 slice. The times are simulated.
256 devices in a mesh: src: 16 (over y, x), tgt: 16 (over z, core).
Axes of the slice: x: 4, y: 4, z: 8, core: 2. Of those that a mesh axis runs over, the one named last changes fastest.
Arguments:
- src_feat: bfloat16 [64, 131072], P(None, ('src', 'tgt')), may hold values from -0.375 to 0.375
- tgt_feat: bfloat16 [64, 131072], P(None, ('tgt', 'src')), may hold values from -0.375 to 0.375
- row_pot: float32 [131072], P(('src', 'tgt')), may hold values from -1 to 1
- col_pot: float32 [131072], P(('tgt', 'src')), may hold values from -1 to 1
- src_mass: float32 [131072], P(('src', 'tgt')), may hold values from 2 to 20
- tgt_mass: float32 [131072], P(('tgt', 'src')), may hold values from 2 to 20
- rhs_src: float32 [131072], P(('src', 'tgt')), may hold values from -4 to 4
- rhs_tgt: float32 [131072], P(('tgt', 'src')), may hold values from -4 to 4
- tile_rows: int32 [16, 16, 8], P('src', 'tgt'), may hold values from 0 to 7, as said below
- tile_cols: int32 [16, 16, 8], P('src', 'tgt'), may hold values from 0 to 7
- tile_count: int32 [16, 16], P('src', 'tgt'), may hold values from 1 to 8, as said below
Outputs:
- adjoint_src: float32 [131072], P(('src', 'tgt'))
- adjoint_tgt: float32 [131072], P(('tgt', 'src'))
- grad_src: float32 [64, 131072], P(None, ('src', 'tgt'))
- grad_tgt: float32 [64, 131072], P(None, ('tgt', 'src'))
Inputs may be any that keep to these rules, and one draw needn't show every extreme that they name: `tile_rows`: the first tile_count slots of a grid position name distinct pairs of source and target blocks; later slots are unused. `tile_count`: some grid position holds exactly 8 tiles.
All inputs are finite; a program needn't handle non-finite values.
Results may differ from a plain program's by a relative error of at most 0.0005.
Values may be sent and summed in bfloat16 or wider, within the bound.
No kernel may reach another device: no remote copies, remote signals or barrier semaphores. Data moves between devices by JAX's collectives and lax.ppermute only.
A program may use at most 128 MiB of HBM per device.

v0:
```python
import jax
import jax.numpy as jnp
from jax import lax
from jax.sharding import PartitionSpec as P

TILE = 1024
ITERS = 3


EPS = 0.05
RHO = 1.0


def add_into(total, start, piece, axis):
    current = lax.dynamic_slice_in_dim(total, start, piece.shape[axis], axis)
    return lax.dynamic_update_slice_in_dim(total, current + piece, start, axis)


def kernel_block(src_block, tgt_block, row_block, col_block):
    products = lax.dot_general(
        src_block, tgt_block, (((0,), (0,)), ((), ())), preferred_element_type=jnp.float32
    )
    return jnp.exp((row_block[:, None] + col_block[None, :] + 2.0 * products) / EPS)


def inner_local(left, right):
    return jnp.sum(left[0] * right[0]) + jnp.sum(left[1] * right[1])


def combine(left, right, factor):
    return (left[0] + factor * right[0], left[1] + factor * right[1])


def residual_squares(vector):
    return lax.psum(inner_local(vector, vector), ("src", "tgt"))


def shards(
    src_feat,
    tgt_feat,
    row_pot,
    col_pot,
    src_mass,
    tgt_mass,
    rhs_src,
    rhs_tgt,
    tile_rows,
    tile_cols,
    tile_count,
):
    src_wide = src_feat.astype(jnp.float32)
    tgt_wide = tgt_feat.astype(jnp.float32)
    row_term = row_pot - jnp.sum(src_wide * src_wide, axis=0)
    col_term = col_pot - jnp.sum(tgt_wide * tgt_wide, axis=0)
    src_all = lax.all_gather(src_feat, "tgt", axis=1, tiled=True)
    tgt_all = lax.all_gather(tgt_feat, "src", axis=1, tiled=True)
    row_all = lax.all_gather(row_term, "tgt", axis=0, tiled=True)
    col_all = lax.all_gather(col_term, "src", axis=0, tiled=True)
    src_len = src_all.shape[1]
    tgt_len = tgt_all.shape[1]
    live_count = tile_count[0, 0]
    row_ids = tile_rows[0, 0]
    col_ids = tile_cols[0, 0]

    def starts(slot_index):
        return (row_ids[slot_index] * TILE, col_ids[slot_index] * TILE)

    def build(slot_index):
        row_start, col_start = starts(slot_index)
        kernel = kernel_block(
            lax.dynamic_slice_in_dim(src_all, row_start, TILE, 1),
            lax.dynamic_slice_in_dim(tgt_all, col_start, TILE, 1),
            lax.dynamic_slice_in_dim(row_all, row_start, TILE, 0),
            lax.dynamic_slice_in_dim(col_all, col_start, TILE, 0),
        )
        return (kernel, row_start, col_start)

    def sweep(update, initial):

        def visit(slot_index, running):
            kernel, row_start, col_start = build(slot_index)
            return update(running, kernel, row_start, col_start)

        return lax.fori_loop(0, live_count, visit, initial)

    def spread_src(vector):
        return lax.all_gather(vector, "tgt", axis=0, tiled=True)

    def spread_tgt(vector):
        return lax.all_gather(vector, "src", axis=0, tiled=True)

    def product_update(src_full, tgt_full):

        def update(running, kernel, row_start, col_start):
            tgt_piece = lax.dynamic_slice_in_dim(tgt_full, col_start, TILE, 0)
            src_piece = lax.dynamic_slice_in_dim(src_full, row_start, TILE, 0)
            return (
                add_into(
                    running[0],
                    row_start,
                    jnp.dot(kernel, tgt_piece, precision=lax.Precision.HIGHEST),
                    0,
                ),
                add_into(
                    running[1],
                    col_start,
                    jnp.dot(src_piece, kernel, precision=lax.Precision.HIGHEST),
                    0,
                ),
            )

        return update

    def margin_update(running, kernel, row_start, col_start):
        return (
            add_into(running[0], row_start, jnp.sum(kernel, axis=1), 0),
            add_into(running[1], col_start, jnp.sum(kernel, axis=0), 0),
        )

    zero_rows = jnp.zeros((src_len,), jnp.float32)
    zero_cols = jnp.zeros((tgt_len,), jnp.float32)
    damp_src = EPS / RHO * src_mass * jnp.exp(-row_pot / RHO)
    damp_tgt = EPS / RHO * tgt_mass * jnp.exp(-col_pot / RHO)

    def apply(pair, diags):
        src_full = spread_src(pair[0])
        tgt_full = spread_tgt(pair[1])
        row_acc, col_acc = sweep(product_update(src_full, tgt_full), (zero_rows, zero_cols))
        row_out = lax.psum_scatter(row_acc, "tgt", scatter_dimension=0, tiled=True)
        col_out = lax.psum_scatter(col_acc, "src", scatter_dimension=0, tiled=True)
        return (diags[0] * pair[0] + row_out, diags[1] * pair[1] + col_out)

    rhs_pair = (rhs_src, rhs_tgt)
    row_sums, col_sums = sweep(margin_update, (zero_rows, zero_cols))
    row_marg = lax.psum_scatter(row_sums, "tgt", scatter_dimension=0, tiled=True)
    col_marg = lax.psum_scatter(col_sums, "src", scatter_dimension=0, tiled=True)
    diags = (row_marg + damp_src, col_marg + damp_tgt)
    first_image = apply(rhs_pair, diags)
    solution = (jnp.zeros_like(rhs_src), jnp.zeros_like(rhs_tgt))
    residual = rhs_pair
    direction = residual
    norm_now = residual_squares(residual)
    for step in range(ITERS):
        image = first_image if step == 0 else apply(direction, diags)
        alpha = norm_now / lax.psum(inner_local(direction, image), ("src", "tgt"))
        solution = combine(solution, direction, alpha)
        residual = combine(residual, image, -alpha)
        norm_next = residual_squares(residual)
        direction = combine(residual, direction, norm_next / norm_now)
        norm_now = norm_next
    adjoint_src, adjoint_tgt = solution
    src_full = spread_src(adjoint_src)
    tgt_full = spread_tgt(adjoint_tgt)
    feats = src_feat.shape[0]

    def grad_update(running, kernel, row_start, col_start):
        row_w, row_wy, col_w, col_wx = running
        src_block = lax.dynamic_slice_in_dim(src_all, row_start, TILE, 1)
        tgt_block = lax.dynamic_slice_in_dim(tgt_all, col_start, TILE, 1)
        weights = kernel * (
            lax.dynamic_slice_in_dim(src_full, row_start, TILE, 0)[:, None]
            + lax.dynamic_slice_in_dim(tgt_full, col_start, TILE, 0)[None, :]
        )
        narrow = weights.astype(jnp.bfloat16)
        row_w = add_into(row_w, row_start, jnp.sum(weights, axis=1), 0)
        col_w = add_into(col_w, col_start, jnp.sum(weights, axis=0), 0)
        row_wy = add_into(
            row_wy,
            row_start,
            lax.dot_general(
                tgt_block, narrow, (((1,), (1,)), ((), ())), preferred_element_type=jnp.float32
            ),
            1,
        )
        col_wx = add_into(
            col_wx, col_start, jnp.dot(src_block, narrow, preferred_element_type=jnp.float32), 1
        )
        return (row_w, row_wy, col_w, col_wx)

    row_w, row_wy, col_w, col_wx = sweep(
        grad_update,
        (
            zero_rows,
            jnp.zeros((feats, src_len), jnp.float32),
            zero_cols,
            jnp.zeros((feats, tgt_len), jnp.float32),
        ),
    )
    row_wy_sum, row_w_sum = (
        lax.psum_scatter(row_wy, "tgt", scatter_dimension=1, tiled=True),
        lax.psum_scatter(row_w, "tgt", scatter_dimension=0, tiled=True),
    )
    col_wx_sum, col_w_sum = (
        lax.psum_scatter(col_wx, "src", scatter_dimension=1, tiled=True),
        lax.psum_scatter(col_w, "src", scatter_dimension=0, tiled=True),
    )
    grad_src = 2.0 / EPS * (src_wide * row_w_sum[None, :] - row_wy_sum)
    grad_tgt = 2.0 / EPS * (tgt_wide * col_w_sum[None, :] - col_wx_sum)
    return (adjoint_src, adjoint_tgt, grad_src, grad_tgt)


def solution(mesh):
    in_specs = (
        P(None, ("src", "tgt")),
        P(None, ("tgt", "src")),
        P(("src", "tgt")),
        P(("tgt", "src")),
        P(("src", "tgt")),
        P(("tgt", "src")),
        P(("src", "tgt")),
        P(("tgt", "src")),
        P("src", "tgt", None),
        P("src", "tgt", None),
        P("src", "tgt"),
    )
    out_specs = (
        P(("src", "tgt")),
        P(("tgt", "src")),
        P(None, ("src", "tgt")),
        P(None, ("tgt", "src")),
    )
    return jax.shard_map(shards, mesh=mesh, in_specs=in_specs, out_specs=out_specs, check_vma=False)
```

profile of v0, /device:TPU:24, one launch (start us, length us, event | category | flops | bytes accessed | tf_op | source)
XLA Modules:
  0.0 1637.0 jit_solution(10796461105086732582)
XLA Ops:
  11.8 23.0 %all-gather.1 = f32[16,1,512]{2,1,0:T(1,128)S(1)} all-gather(f32[1,1,512]{2,1,0:T(1,128)S(1)} %bitcast.146), channel_id=1, replica_groups=mesh['src'=16,'tgt'=16] {'src'}, dimensions={0}, use_global_device_ids=true | all-gather | bytes 34816 | tf_op jit(solution)/shard_map/all_gather | solution.py:58
  34.8 21.1 %all-gather.2 = f32[16,1,512]{2,1,0:T(1,128)S(1)} all-gather(f32[1,1,512]{2,1,0:T(1,128)} %bitcast.137), channel_id=1, replica_groups=mesh['src'=16,'tgt'=16] {'src'}, dimensions={0}, use_global_device_ids=true | all-gather | bytes 34816 | tf_op jit(solution)/shard_map/all_gather | solution.py:90
  100.3 28.1 %while.64 = (s32[]{:T(128)}, f32[8192]{0:T(1024)S(1)}, f32[8192]{0:T(1024)S(1)}, s32[]{:T(128)}, s32[8]{0:T(128)}, /*index=5*/f32[8192]{0:T(1024)S(1)}, s32[8]{0...) while((s32[]{:T(128)}, f32[8192]{0:T(1024)S(1)}, ...), condition=%wide.region_8.0_spmd, body=%wide.region_5.8_spmd.sunk | while | flops 140509200 | bytes 319811 | solution.py:84
  129.0 55.4 %while.65 = (s32[]{:T(128)}, f32[8192]{0:T(1024)S(1)}, f32[8192]{0:T(1024)S(1)}, s32[]{:T(128)}, s32[8]{0:T(128)}, /*index=5*/f32[8192]{0:T(1024)S(1)}, s32[8]{0...) while((s32[]{:T(128)}, f32[8192]{0:T(1024)S(1)}, ...), condition=%wide.region_11.0_spmd, body=%wide.region_10.0_spmd.sunk | while | flops 167774224 | bytes 12935515 | solution.py:84
  187.7 178.3 %all-reduce.16.cloned.1.call-done = (f32[8192]{0:T(1024)}, f32[8192]{0:T(1024)}) async-done(((f32[8192]{0:T(1024)}, f32[8192]{0:T(1024)}), (f32[8192]{0:T(1024)}, f32[8192]{0:T(1024)})) %all-reduce.16.cloned.1.call-update) | async-done | bytes 65552
  367.4 92.0 %all-reduce.18.cloned.1.call-done = (f32[8192]{0:T(1024)}, f32[8192]{0:T(1024)}) async-done(((f32[8192]{0:T(1024)}, f32[8192]{0:T(1024)}), (f32[8192]{0:T(1024)}, f32[8192]{0:T(1024)})) %all-reduce.18.cloned.1.call-update) | async-done | bytes 65552
  463.4 73.7 %all-reduce.10 = (f32[]{:T(128)}, f32[]{:T(128)}) all-reduce(f32[]{:T(128)S(6)} %add.352, f32[]{:T(128)S(6)} %add.357), channel_id=1, replica_groups=mesh['src'=16,'tgt'=16] {'src','tgt'}, use_global_device_ids=true, to_apply=%region_2.3 | all-reduce | flops 2 | bytes 16 | tf_op jit(solution)/shard_map/psum | solution.py:35
  541.1 74.9 %psum.44 = f32[]{:T(128)} all-reduce(f32[]{:T(128)S(6)} %add.360), channel_id=1, replica_groups=mesh['src'=16,'tgt'=16] {'src','tgt'}, use_global_device_ids=true, to_apply=%region_20.0 | all-reduce | flops 1 | bytes 8 | tf_op jit(solution)/shard_map/psum | solution.py:35
  632.9 21.4 %all-gather.4 = f32[16,1,512]{2,1,0:T(1,128)S(1)} all-gather(f32[1,1,512]{2,1,0:T(1,128)S(1)} %bitcast.140), channel_id=1, replica_groups=mesh['src'=16,'tgt'=16] {'src'}, dimensions={0}, use_global_device_ids=true | all-gather | bytes 34816 | tf_op jit(solution)/shard_map/all_gather | solution.py:90
  654.3 55.4 %while.66 = (s32[]{:T(128)}, f32[8192]{0:T(1024)S(1)}, f32[8192]{0:T(1024)S(1)}, s32[]{:T(128)}, s32[8]{0:T(128)}, /*index=5*/f32[8192]{0:T(1024)S(1)}, s32[8]{0...) while((s32[]{:T(128)}, f32[8192]{0:T(1024)S(1)}, ...), condition=%wide.region_22.0_spmd, body=%wide.region_21.0_spmd.sunk | while | flops 167774224 | bytes 12935515 | solution.py:84
  709.7 118.6 %all-reduce.5 = f32[8192]{0:T(1024)S(1)} all-reduce(f32[8192]{0:T(1024)S(1)} %get-tuple-element.331), channel_id=7, replica_groups=mesh['src'=16,'tgt'=16] {'src'}, use_global_device_ids=true, to_apply=%region_25.0.clone | all-reduce | flops 8192 | bytes 65536
  829.0 45.7 %all-reduce.4 = f32[8192]{0:T(1024)S(1)} all-reduce(f32[8192]{0:T(1024)S(1)} %get-tuple-element.330), channel_id=6, replica_groups=mesh['src'=16,'tgt'=16] {'tgt'}, use_global_device_ids=true, to_apply=%region_23.0.clone | all-reduce | flops 8192 | bytes 65536
  876.6 78.5 %psum.45 = f32[]{:T(128)} all-reduce(f32[]{:T(128)S(6)} %add.365), channel_id=1, replica_groups=mesh['src'=16,'tgt'=16] {'src','tgt'}, use_global_device_ids=true, to_apply=%region_27.0 | all-reduce | flops 1 | bytes 8 | tf_op jit(solution)/shard_map/psum | solution.py:145
  958.9 74.2 %psum.46 = f32[]{:T(128)} all-reduce(f32[]{:T(128)S(6)} %add.369), channel_id=1, replica_groups=mesh['src'=16,'tgt'=16] {'src','tgt'}, use_global_device_ids=true, to_apply=%region_30.0 | all-reduce | flops 1 | bytes 8 | tf_op jit(solution)/shard_map/psum | solution.py:35
  1034.5 20.8 %all-gather.6 = f32[16,1,512]{2,1,0:T(1,128)S(1)} all-gather(f32[1,1,512]{2,1,0:T(1,128)S(1)} %bitcast.142), channel_id=1, replica_groups=mesh['src'=16,'tgt'=16] {'src'}, dimensions={0}, use_global_device_ids=true | all-gather | bytes 34816 | tf_op jit(solution)/shard_map/all_gather | solution.py:90
  1070.7 55.6 %while.67 = (s32[]{:T(128)}, f32[8192]{0:T(1024)S(1)}, f32[8192]{0:T(1024)S(1)}, s32[]{:T(128)}, s32[8]{0:T(128)}, /*index=5*/f32[8192]{0:T(1024)S(1)}, s32[8]{0...) while((s32[]{:T(128)}, f32[8192]{0:T(1024)S(1)}, ...), condition=%wide.region_32.0_spmd, body=%wide.region_31.0_spmd.sunk | while | flops 167774224 | bytes 12935515 | solution.py:84
  1126.4 119.2 %all-reduce.7 = f32[8192]{0:T(1024)S(1)} all-reduce(f32[8192]{0:T(1024)S(1)} %get-tuple-element.333), channel_id=9, replica_groups=mesh['src'=16,'tgt'=16] {'src'}, use_global_device_ids=true, to_apply=%region_35.0.clone | all-reduce | flops 8192 | bytes 65536
  1246.2 45.7 %all-reduce.6 = f32[8192]{0:T(1024)S(1)} all-reduce(f32[8192]{0:T(1024)S(1)} %get-tuple-element.332), channel_id=8, replica_groups=mesh['src'=16,'tgt'=16] {'tgt'}, use_global_device_ids=true, to_apply=%region_33.0.clone | all-reduce | flops 8192 | bytes 65536
  1293.9 78.5 %psum.47 = f32[]{:T(128)} all-reduce(f32[]{:T(128)S(6)} %add.374), channel_id=1, replica_groups=mesh['src'=16,'tgt'=16] {'src','tgt'}, use_global_device_ids=true, to_apply=%region_37.0 | all-reduce | flops 1 | bytes 8 | tf_op jit(solution)/shard_map/psum | solution.py:145
  1373.8 20.7 %all-gather.9 = f32[16,1,512]{2,1,0:T(1,128)S(1)} all-gather(f32[1,1,512]{2,1,0:T(1,128)S(1)} %bitcast.143), channel_id=1, replica_groups=mesh['src'=16,'tgt'=16] {'src'}, dimensions={0}, use_global_device_ids=true | all-gather | bytes 34816 | tf_op jit(solution)/shard_map/all_gather | solution.py:90
  1412.3 40.4 %while.68 = (s32[]{:T(128)}, f32[8192]{0:T(1024)S(1)}, f32[64,8192]{1,0:T(8,128)}, f32[8192]{0:T(1024)S(1)}, f32[64,8192]{1,0:T(8,128)S(1)}, /*index=5*/s32[]{:T...) while((s32[]{:T(128)}, f32[8192]{0:T(1024)S(1)}, ...), condition=%wide.region_41.0_spmd, body=%wide.region_38.0_spmd.sunk | while | flops 412221440 | bytes 7946619 | solution.py:84
  1454.0 80.1 %all-reduce.8 = f32[8192]{0:T(1024)S(1)} all-reduce(f32[8192]{0:T(1024)S(1)} %get-tuple-element.334), channel_id=10, replica_groups=mesh['src'=16,'tgt'=16] {'tgt'}, use_global_device_ids=true, to_apply=%region_42.0.clone | all-reduce | flops 8192 | bytes 65536
  1534.2 72.1 %all-reduce.9 = f32[8192]{0:T(1024)S(1)} all-reduce(f32[8192]{0:T(1024)S(1)} %get-tuple-element.336), channel_id=12, replica_groups=mesh['src'=16,'tgt'=16] {'src'}, use_global_device_ids=true, to_apply=%region_44.0.clone | all-reduce | flops 8192 | bytes 65536
  1607.9 20.7 %reduce-scatter.5.cloned.1.call-done = f32[64,512]{1,0:T(8,128)} async-done(((f32[64,8192]{1,0:T(8,128)}), f32[64,512]{1,0:T(8,128)}) %reduce-scatter.5.cloned.1.call-update) | async-done | bytes 131088 | tf_op jit(solution)/shard_map/reduce_scatter | solution.py:194
  (279 shorter events, 303.7 us)
Async XLA Ops:
  7.2 83.5 %all-gather.13.cloned.1.call-start = ((), (), s32[]{:S(2)}) async-start(), calls=%async_computation.2 | async-start | bytes 1114112 | tf_op jit(solution)/shard_map/all_gather | solution.py:55
  7.9 92.4 %all-gather.15.cloned.1.call-start = ((), (), s32[]{:S(2)}) async-start(), calls=%async_computation.3 | async-start | bytes 1114112 | tf_op jit(solution)/shard_map/all_gather | solution.py:56
  8.6 357.3 %all-reduce.16.cloned.1.call-start = ((), (), s32[]{:S(2)}) async-start(), calls=%async_computation.6 | async-start | bytes 131072
  128.4 0.6 copy-start.3
  128.4 0.6 copy-start.4
  128.4 56.7 %copy-start.18 = (u32[256]{0:T(256)S(1)}, u32[256]{0:T(256)}, u32[]{:S(2)}) copy-start(u32[256]{0:T(256)} %constant.113) | copy-start | bytes 3076
  128.5 57.3 %copy-start.17 = (u32[256]{0:T(256)S(1)}, u32[256]{0:T(256)}, u32[]{:S(2)}) copy-start(u32[256]{0:T(256)} %constant.105) | copy-start | bytes 3076
  128.5 237.5 %copy-start.8 = (f32[512]{0:T(512)S(1)}, f32[512]{0:T(512)}, u32[]{:S(2)}) copy-start(f32[512]{0:T(512)} %param.27) | copy-start | bytes 6148
  128.5 237.5 %copy-start.9 = (f32[512]{0:T(512)S(1)}, f32[512]{0:T(512)}, u32[]{:S(2)}) copy-start(f32[512]{0:T(512)} %param.23) | copy-start | bytes 6148
  128.5 237.5 %copy-start.13 = (f32[512]{0:T(512)S(1)}, f32[512]{0:T(512)}, u32[]{:S(2)}) copy-start(f32[512]{0:T(512)} %param.25) | copy-start | bytes 6148
  128.5 330.9 %copy-start.7 = (f32[512]{0:T(512)S(1)}, f32[512]{0:T(512)}, u32[]{:S(2)}) copy-start(f32[512]{0:T(512)} %param.28) | copy-start | bytes 6148
  128.5 330.9 %copy-start.10 = (f32[512]{0:T(512)S(1)}, f32[512]{0:T(512)}, u32[]{:S(2)}) copy-start(f32[512]{0:T(512)} %param.24) | copy-start | bytes 6148
  128.5 330.9 %copy-start.14 = (f32[512]{0:T(512)S(1)}, f32[512]{0:T(512)}, u32[]{:S(2)}) copy-start(f32[512]{0:T(512)} %param.26) | copy-start | bytes 6148
  184.5 3.2 copy-start.5
  185.1 274.4 %all-reduce.18.cloned.1.call-start = ((), (), s32[]{:S(2)}) async-start(), calls=%async_computation.7 | async-start | bytes 131072
  187.6 1418.7 %reduce-scatter.3.cloned.1.call-start = ((), (), s32[]{:S(2)}) async-start(), calls=%async_computation.4 | async-start | bytes 2228224 | tf_op jit(solution)/shard_map/reduce_scatter | solution.py:190
  1126.4 285.9 %copy-start.15 = (s32[8]{0:T(128)S(1)}, s32[8]{0:T(128)}, u32[]{:S(2)}) copy-start(s32[8]{0:T(128)} %get-tuple-element.1208) | copy-start | bytes 100
  1126.4 285.9 %copy-start.16 = (s32[8]{0:T(128)S(1)}, s32[8]{0:T(128)}, u32[]{:S(2)}) copy-start(s32[8]{0:T(128)} %get-tuple-element.1212) | copy-start | bytes 100
  1373.7 38.5 %copy-start.11 = (f32[512]{0:T(512)}, f32[512]{0:T(512)S(1)}, u32[]{:S(2)}) copy-start(f32[512]{0:T(512)S(1)} %multiply_add_fusion) | copy-start | bytes 6148
  1373.8 38.5 %copy-start.12 = (f32[512]{0:T(512)}, f32[512]{0:T(512)S(1)}, u32[]{:S(2)}) copy-start(f32[512]{0:T(512)S(1)} %multiply_add_fusion.1) | copy-start | bytes 6148
  1452.7 1.4 copy-start
  1452.7 153.7 %copy-start.1 = (bf16[64,512]{1,0:T(8,128)(2,1)S(1)}, bf16[64,512]{1,0:T(8,128)(2,1)}, u32[]{:S(2)}) copy-start(bf16[64,512]{1,0:T(8,128)(2,1)} %param.21) | copy-start | bytes 196612
  1452.7 175.9 %copy-start.2 = (bf16[64,512]{1,0:T(8,128)(2,1)S(1)}, bf16[64,512]{1,0:T(8,128)(2,1)}, u32[]{:S(2)}) copy-start(bf16[64,512]{1,0:T(8,128)(2,1)} %param.22) | copy-start | bytes 196612
  1452.7 175.9 %reduce-scatter.5.cloned.1.call-start = ((), (), s32[]{:S(2)}) async-start(), calls=%async_computation.5 | async-start | bytes 2228224 | tf_op jit(solution)/shard_map/reduce_scatter | solution.py:194
  (1 other events, 0.6 us)
Sparse Core Ops, SparseCore 0:
  9.8 41.2 all-gather.12
  53.5 46.7 all-gather.14
  185.2 180.7 all-reduce.15
  369.9 89.4 all-reduce.17
  1452.8 94.9 reduce-scatter.2
  1551.3 77.2 reduce-scatter.4
where the time goes:
time: 1640 us
  blocking collectives  1050 us (64%)
  waiting for transfers between devices  302 us (18%)
  matrix products  145 us (9%)
  local copies, waits for them, and re-layouts  50.6 us (3%)
  loops' own time  44.1 us (3%)
  between operations  30.2 us (2%)
    unnamed x6, blocking collectives  481 us
    unnamed x8, waiting for transfers between devices  272 us
    psum x3, blocking collectives, residual_squares(): return lax.psum(inner_local(vector, vector), ('src', 'tgt'))  223 us
    psum x2, blocking collectives, shards(): alpha = norm_now / lax.psum(inner_local(direction, image), ('src', 'tgt'))  157 us
    all_gather x4, blocking collectives, spread_tgt(): return lax.all_gather(vector, 'src', axis=0, tiled=True)  83.9 us
    all_gather x4, blocking collectives, spread_src(): return lax.all_gather(vector, 'tgt', axis=0, tiled=True)  61.8 us
    dot_general x12, matrix products, update(): jnp.dot(kernel, tgt_piece, precision=lax.Precision.HIGHEST)  53.9 us
    dynamic_slice x40, local copies, waits for them, and re-layouts, starts(): return (row_ids[slot_index] * TILE, col_ids[slot_index] * TILE)  44.5 us
  transfers between devices with their start and end apart: 6, of which 4 were waited for; matrix products, arithmetic and copies ran while one was open for 0% of the time, Pallas kernels for 0%

commit v1 on v0

v1 whole, which is shorter than its diff:
```python
import math

import jax
import jax.numpy as jnp
from jax import lax
from jax.experimental import pallas as pl
from jax.experimental.pallas import tpu as pltpu
from jax.sharding import PartitionSpec as P

TILE = 1024
FEATS = 64
LANES = 128
BLOCKS = 8
SLOTS = 8
PART = 512
EPS = 0.05
RHO = 1.0
TERM_SCALE = math.log2(math.e) / EPS
DOWN = 2.0**-40
UP = 2.0**40
F32 = jnp.float32
BF16 = jnp.bfloat16
VMEM = pl.BlockSpec(memory_space=pltpu.VMEM)
SMEM = pl.BlockSpec(memory_space=pltpu.SMEM)
ANY = pl.BlockSpec(memory_space=pl.ANY)
HBM = pl.BlockSpec(memory_space=pltpu.HBM)
RING = (0, -1, 1, -2, 2, -3, 3, 4)
QUAD = (0, 1, -1, 2)


def params(mib):
    return pltpu.CompilerParams(vmem_limit_bytes=mib * 2**20)


def shape(dims, dtype=F32):
    return jax.ShapeDtypeStruct(dims, dtype)


def split3(value):
    high = value.astype(BF16).astype(F32)
    rest = value - high
    middle = rest.astype(BF16).astype(F32)
    low = (rest - middle).astype(BF16).astype(F32)
    return high, middle, low


def payload_kernel(*refs):
    sources, (out_s, out_t), held, sems = refs[:8], refs[8:10], refs[10:18], refs[18]
    copies = [
        pltpu.make_async_copy(source, place, sems.at[i])
        for i, (source, place) in enumerate(zip(sources, held))
    ]
    for copy in copies:
        copy.start()
    for copy in copies:
        copy.wait()
    sf, tf, rp, cp, sm, tm, rs, rt = held
    for feat, pot, mass, rhs, out, first in (
        (sf, rp, sm, rs, out_s, True),
        (tf, cp, tm, rt, out_t, False),
    ):
        wide = feat[...].astype(F32)
        potential = pot[...]
        term = (potential - jnp.sum(wide * wide, axis=0, keepdims=True)) * TERM_SCALE
        damp = EPS / RHO * mass[...] * jnp.exp(-potential / RHO)
        ones = jnp.ones((3, PART), F32)
        pieces = list(split3(term))
        rows = pieces + [ones] if first else [ones] + pieces
        rows += list(split3(rhs[...])) + list(split3(damp))
        rows.append(jnp.zeros((4, PART), F32))
        out[0:FEATS, :] = feat[...]
        out[FEATS : FEATS + 16, :] = jnp.concatenate(rows, axis=0).astype(BF16)


def three(rows, start):
    return rows[start : start + 1] + (rows[start + 1 : start + 2] + rows[start + 2 : start + 3])


def column_of(row):
    return jnp.broadcast_to(row, (LANES, TILE)).T


def lane_sum(partial):
    return jnp.sum(partial.T, axis=0, keepdims=True)


def lane_blocks(row, height):
    return [
        jnp.broadcast_to(row[:, LANES * l : LANES * (l + 1)], (height, LANES))
        for l in range(TILE // LANES)
    ]


def add_row(ref, index, row):
    ref[pl.ds(index, 1), :] = ref[pl.ds(index, 1), :] + row


def total(values):
    result = values[0]
    for value in values[1:]:
        result = result + value
    return result


def pair_of(ref, block):
    return jnp.concatenate([ref[2 * block], ref[2 * block + 1]], axis=1)


def ring_block(me, dz, other):
    place = lax.rem(me // 2 + (dz + 8), 8)
    core = lax.rem(me, 2)
    return 2 * place + (1 - core if other else core)


def quad_block(me, dy, dx):
    return 4 * lax.rem(me // 4 + (dy + 4), 4) + lax.rem(lax.rem(me, 4) + (dx + 4), 4)


def build_kernel(
    meta, s0, s1, t0, t1, t2, t3, t4,
    kern, xs, ys, bp, bq, dp, dq, rsum, csum,
    left, right, sums, prods, pcol, sems,
):
    me_s, me_t = meta[17], meta[18]
    copies = []
    for k in range(8):
        for other, stack in enumerate((s0, s1)):
            copies.append((stack.at[k], xs.at[ring_block(me_t, RING[k], other)]))
    for k in range(4):
        far = (t3.at[k] if k < 2 else t4.at[k - 2])
        for dx, piece in ((0, t0.at[k]), (1, t2.at[k]), (-1, t1.at[k]), (2, far)):
            copies.append((piece, ys.at[quad_block(me_s, QUAD[k], dx)]))
    copies = [
        pltpu.make_async_copy(source, place, sems.at[i])
        for i, (source, place) in enumerate(copies)
    ]
    for copy in copies:
        copy.start()
    rsum[...] = jnp.zeros_like(rsum)
    csum[...] = jnp.zeros_like(csum)
    for copy in copies:
        copy.wait()
    for block in range(BLOCKS):
        for ref, vec, damp in ((xs, bp, dp), (ys, bq, dq)):
            for side in range(2):
                rows = ref[2 * block + side, FEATS : FEATS + 16, :].astype(F32)
                cells = slice(PART * side, PART * (side + 1))
                vec[block : block + 1, cells] = three(rows, 6)
                damp[block : block + 1, cells] = three(rows, 9)

    def tile(slot, carry):
        rb, cb = meta[slot], meta[8 + slot]
        x = pair_of(xs, rb)
        y = pair_of(ys, cb)
        keep = lax.broadcasted_iota(jnp.int32, (16, TILE), 0) < 6
        xt = jnp.where(keep, x[FEATS:].astype(F32), 0.0)
        yt = jnp.where(keep, y[FEATS:].astype(F32), 0.0)
        scaled = x[:FEATS].astype(F32) * (2.0 * TERM_SCALE)
        zeros = jnp.zeros((48, TILE), F32)
        left[...] = jnp.concatenate([*split3(scaled), xt, zeros], axis=0).astype(BF16).T
        yf = y[:FEATS]
        right[...] = jnp.concatenate(
            [yf, yf, yf, jnp.concatenate([yt, zeros], axis=0).astype(BF16)], axis=0
        )
        for strip in range(4):
            cells = slice(256 * strip, 256 * (strip + 1))
            kern[slot, :, cells] = jnp.dot(
                left[...], right[:, cells], preferred_element_type=F32
            )
        q = lane_blocks(bq[pl.ds(cb, 1), :], 8)
        pcol[...] = column_of(bp[pl.ds(rb, 1), :])
        count = TILE // LANES

        def rows_of(step, accs):
            csums, cprods = accs
            for u in range(4):
                at = pl.ds(pl.multiple_of(step * 32 + 8 * u, 8), 8)
                ks = [
                    jnp.exp2(kern[slot, at, LANES * l : LANES * (l + 1)]) for l in range(count)
                ]
                for l in range(count):
                    kern[slot, at, LANES * l : LANES * (l + 1)] = ks[l]
                p = pcol[at, :]
                sums[at, :] = total(ks)
                prods[at, :] = total([ks[l] * q[l] for l in range(count)])
                csums = tuple(csums[l] + ks[l] for l in range(count))
                cprods = tuple(cprods[l] + ks[l] * p for l in range(count))
            return csums, cprods

        zero = tuple(jnp.zeros((8, LANES), F32) for l in range(count))
        csums, cprods = lax.fori_loop(0, TILE // 32, rows_of, (zero, zero))
        add_row(rsum, rb, lane_sum(sums[...]))
        add_row(rsum, 8 + rb, lane_sum(prods[...]))
        add_row(csum, cb, jnp.sum(jnp.concatenate(csums, axis=1), axis=0, keepdims=True))
        add_row(csum, 8 + cb, jnp.sum(jnp.concatenate(cprods, axis=1), axis=0, keepdims=True))
        return carry

    lax.fori_loop(0, meta[16], tile, 0)


def lane_partial(value):
    rows = jnp.sum(value, axis=0, keepdims=True)
    return total([rows[:, LANES * l : LANES * (l + 1)] for l in range(TILE // LANES)])


def lane_largest(value):
    rows = jnp.max(value, axis=0, keepdims=True)
    result = rows[:, :LANES]
    for l in range(1, TILE // LANES):
        result = jnp.maximum(result, rows[:, LANES * l : LANES * (l + 1)])
    return result


def scalar(row):
    return jnp.sum(row, axis=1, keepdims=True)


def both_of(pieces):
    return pieces[0][...] + pieces[1][...]


def unpack(value):
    return jnp.concatenate(
        [value[BLOCKS * l : BLOCKS * (l + 1)] for l in range(TILE // LANES)], axis=1
    )


def pack_into(out, value):
    for l in range(TILE // LANES):
        out[BLOCKS * l : BLOCKS * (l + 1), :] = value[:, LANES * l : LANES * (l + 1)]


def apply_kernel(
    meta, r0, r1, c0, c1, bp, bq, dp, dq, kern,
    v1p, v1q, gp, gq, rout, cout,
    prods, pcol, rimg, cimg,
):
    rows = both_of((r0, r1))
    cols = both_of((c0, c1))
    gp[...] = rows[:8] + dp[...]
    gq[...] = cols[:8] + dq[...]
    v1p[...] = gp[...] * (bp[...] * DOWN) + rows[8:] * DOWN
    v1q[...] = gq[...] * (bq[...] * DOWN) + cols[8:] * DOWN
    rimg[...] = jnp.zeros_like(rimg)
    cimg[...] = jnp.zeros_like(cimg)
    for b, v, g, out in ((bp, v1p, gp, cout), (bq, v1q, gq, rout)):
        out[64:72, :] = jnp.zeros((8, LANES), F32)
        for place, value in enumerate(
            (
                lane_partial(b[...] * b[...]),
                lane_partial(b[...] * v[...]),
                lane_partial(v[...] * v[...]),
                lane_largest(g[...]),
            )
        ):
            out[64 + place : 65 + place, :] = value
    count = TILE // LANES

    def tile(slot, carry):
        rb, cb = meta[slot], meta[8 + slot]
        q = lane_blocks(v1q[pl.ds(cb, 1), :], 8)
        pcol[...] = column_of(v1p[pl.ds(rb, 1), :])

        def rows_of(step, cprods):
            for u in range(4):
                at = pl.ds(pl.multiple_of(step * 32 + 8 * u, 8), 8)
                ks = [kern[slot, at, LANES * l : LANES * (l + 1)] for l in range(count)]
                p = pcol[at, :]
                prods[at, :] = total([ks[l] * q[l] for l in range(count)])
                cprods = tuple(cprods[l] + ks[l] * p for l in range(count))
            return cprods

        zero = tuple(jnp.zeros((8, LANES), F32) for l in range(count))
        cprods = lax.fori_loop(0, TILE // 32, rows_of, zero)
        add_row(rimg, rb, lane_sum(prods[...]))
        add_row(cimg, cb, jnp.sum(jnp.concatenate(cprods, axis=1), axis=0, keepdims=True))
        return carry

    lax.fori_loop(0, meta[16], tile, 0)
    pack_into(rout, rimg[...])
    pack_into(cout, cimg[...])


def form_kernel(
    meta, r0, r1, c0, c1, bp, bq, v1p, v1q, gp, gq, kern,
    e1p, e1q, wp, wq, hp, hq, dots, known,
    pcol, acc,
):
    rows = both_of((r0, r1))
    cols = both_of((c0, c1))
    both = rows[64:72] + cols[64:72]
    bb, bv, vv, sigma = (scalar(both[i : i + 1]) for i in range(4))
    rows, cols = unpack(rows), unpack(cols)
    inverse = 1.0 / sigma
    lift = UP * inverse
    alpha = bb / (bv * lift)
    dots[...] = jnp.zeros_like(dots)
    known[...] = jnp.zeros_like(known)
    known[0:1, :] = jnp.broadcast_to(bb, (1, LANES))
    known[1:2, :] = jnp.broadcast_to(bv * lift, (1, LANES))
    known[2:3, :] = jnp.broadcast_to((vv * lift) * lift, (1, LANES))
    known[3:4, :] = jnp.broadcast_to(inverse, (1, LANES))
    found = []
    for b, v1, g, image, e1, w, h in (
        (bp, v1p, gp, rows, e1p, wp, hp),
        (bq, v1q, gq, cols, e1q, wq, hq),
    ):
        second = g[...] * v1[...] + image
        first = v1[...] * lift
        next_image = (second * lift) * inverse
        residual = b[...] - alpha * first
        turned = first - alpha * next_image
        e1[...] = residual
        w[...] = turned
        h[...] = first
        found.append(
            (
                lane_partial(residual * residual),
                lane_partial(residual * turned),
                lane_partial(residual * first),
                lane_partial(turned * turned),
                lane_partial(turned * first),
                lane_partial(next_image * turned),
                lane_partial(first * next_image),
                lane_partial((g[...] * inverse) * turned * turned),
            )
        )
    count = TILE // LANES
    acc[...] = jnp.zeros_like(acc)

    def tile(slot, carry):
        rb, cb = meta[slot], meta[8 + slot]
        q = lane_blocks(wq[pl.ds(cb, 1), :] * inverse, 8)
        pcol[...] = column_of(wp[pl.ds(rb, 1), :])

        def rows_of(step, cprods):
            for u in range(4):
                at = pl.ds(pl.multiple_of(step * 32 + 8 * u, 8), 8)
                p = pcol[at, :]
                cprods = tuple(
                    cprods[l] + kern[slot, at, LANES * l : LANES * (l + 1)] * p
                    for l in range(count)
                )
            return cprods

        zero = tuple(jnp.zeros((8, LANES), F32) for l in range(count))
        cprods = lax.fori_loop(0, TILE // 32, rows_of, zero)
        acc[...] = acc[...] + total([cprods[l] * q[l] for l in range(count)])
        return carry

    lax.fori_loop(0, meta[16], tile, 0)
    for place in range(8):
        value = (found[0][place] + found[1][place]) * (1.0 / 16.0)
        if place == 7:
            value = value + 2.0 * jnp.sum(acc[...], axis=0, keepdims=True)
        dots[place : place + 1, :] = value


def grad_kernel(
    meta, q0, q1, known, bp, bq, e1p, e1q, wp, wq, hp, hq, xs, ys, kern,
    adj_s, adj_t, near, far, x0, x1, x2, x3, x4,
    ap, aq, pcol, half, sums, row_w, col_w, row_wy, col_wx,
):
    me_s, me_t = meta[17], meta[18]
    dots = both_of((q0, q1))
    ee, ew, eh, ww, wh, uw, hu, waw = (scalar(dots[i : i + 1]) for i in range(8))
    bb, bh, hh, inverse = (known[i : i + 1, 0:1] for i in range(4))
    alpha1 = bb / bh
    beta1 = ee / bb
    dad = ew + 2.0 * beta1 * eh + beta1 * beta1 * bh
    alpha2 = ee / dad
    e_ad = ew + beta1 * eh
    ad_ad = ww + 2.0 * beta1 * wh + beta1 * beta1 * hh
    rr2 = ee - 2.0 * alpha2 * e_ad + alpha2 * alpha2 * ad_ad
    beta2 = rr2 / ee
    form = waw + 2.0 * beta1 * uw + beta1 * beta1 * hu
    r_ar = ew - 2.0 * alpha2 * (ww + beta1 * wh) + alpha2 * alpha2 * form
    cross = ew + beta1 * eh - alpha2 * ad_ad
    d2_ar2 = cross
    d3ad3 = r_ar + 2.0 * beta2 * d2_ar2 + beta2 * beta2 * dad
    alpha3 = rr2 / d3ad3
    on_b = (alpha1 + alpha2 * beta1 + alpha3 * beta2 * beta1) * inverse
    on_e = (alpha2 + alpha3 * (1.0 + beta2)) * inverse
    on_w = -(alpha3 * alpha2) * inverse
    on_h = on_w * beta1
    ap[...] = on_b * bp[...] + on_e * e1p[...] + on_w * wp[...] + on_h * hp[...]
    aq[...] = on_b * bq[...] + on_e * e1q[...] + on_w * wq[...] + on_h * hq[...]
    for me, vec, out in ((me_t, ap, adj_s), (me_s, aq, adj_t)):
        row = vec[pl.ds(me // 2, 1), :]
        out[...] = jnp.where(me % 2 == 1, row[:, PART:], row[:, :PART])
    row_w[...] = jnp.zeros_like(row_w)
    col_w[...] = jnp.zeros_like(col_w)
    row_wy[...] = jnp.zeros_like(row_wy)
    col_wx[...] = jnp.zeros_like(col_wx)
    count = TILE // LANES

    def tile(slot, carry):
        rb, cb = meta[slot], meta[8 + slot]
        q = lane_blocks(aq[pl.ds(cb, 1), :], 16)
        pcol[...] = column_of(ap[pl.ds(rb, 1), :])

        def rows_of(step, csums):
            for u in range(2):
                at = pl.ds(pl.multiple_of(step * 32 + 16 * u, 16), 16)
                p = pcol[at, :]
                ws = [
                    kern[slot, at, LANES * l : LANES * (l + 1)] * (p + q[l]) for l in range(count)
                ]
                for l in range(count):
                    half[at, LANES * l : LANES * (l + 1)] = ws[l].astype(BF16)
                sums[at, :] = total(ws)
                csums = tuple(csums[l] + (ws[l][:8] + ws[l][8:]) for l in range(count))
            return csums

        zero = tuple(jnp.zeros((8, LANES), F32) for l in range(count))
        csums = lax.fori_loop(0, TILE // 32, rows_of, zero)
        add_row(row_w, rb, lane_sum(sums[...]))
        add_row(col_w, cb, jnp.sum(jnp.concatenate(csums, axis=1), axis=0, keepdims=True))
        x = jnp.concatenate([xs[2 * rb, :FEATS], xs[2 * rb + 1, :FEATS]], axis=1)
        y = jnp.concatenate([ys[2 * cb, :FEATS], ys[2 * cb + 1, :FEATS]], axis=1)
        row_wy[rb] = row_wy[rb] + lax.dot_general(
            y, half[...], (((1,), (1,)), ((), ())), preferred_element_type=F32
        )
        col_wx[cb] = col_wx[cb] + jnp.dot(x, half[...], preferred_element_type=F32)
        return carry

    lax.fori_loop(0, meta[16], tile, 0)

    def part_of(feat, weight, mixed, block):
        wide = feat[block, :FEATS, :].astype(F32)
        row = weight[pl.ds(block // 2, 1), :]
        odd = block % 2 == 1
        mine = jnp.where(odd, row[:, PART:], row[:, :PART])
        whole = mixed[block // 2]
        return (2.0 / EPS) * (wide * mine - jnp.where(odd, whole[:, PART:], whole[:, :PART]))

    for k in range(8):
        for other, out in enumerate((near, far)):
            out[k] = part_of(xs, row_w, row_wy, ring_block(me_t, RING[k], other))
    for k in range(4):
        for dx, out in ((0, x0), (1, x1), (-1, x2), (2, None)):
            part = part_of(ys, col_w, col_wx, quad_block(me_s, QUAD[k], dx))
            if out is None:
                x3[k] = part[:32]
                x4[k] = part[32:]
            else:
                out[k] = part


def swap(value, axis, mask):
    return lax.ppermute(value, axis, [(i, i ^ mask) for i in range(16)])


def along_z(value, step):
    return lax.ppermute(value, "tgt", [(i, (i + 2 * step) % 16) for i in range(16)])


def along_y(value, step):
    return lax.ppermute(value, "src", [(i, (i + 4 * step) % 16) for i in range(16)])


def along_x(value, step):
    return lax.ppermute(value, "src", [(i, i // 4 * 4 + (i + step) % 4) for i in range(16)])


def doubled(value, axis):
    for mask in (1, 2, 4):
        value = value + swap(value, axis, mask)
    return value


def sum_pieces(row, col):
    for mask in (1, 2, 4):
        row, col = row + swap(row, "tgt", mask), col + swap(col, "src", mask)
    return (row, swap(row, "tgt", 8)), (col, swap(col, "src", 8))


def gather_ring(own):
    up = [own]
    down = [own]
    for step in range(4):
        up.append(along_z(up[-1], 1))
        if step < 3:
            down.append(along_z(down[-1], -1))
    stack = jnp.stack([own, up[1], down[1], up[2], down[2], up[3], down[3], up[4]])
    return stack, swap(stack, "tgt", 1)


def gather_quad(own):
    up, down = along_y(own, 1), along_y(own, -1)
    stack = jnp.stack([own, down, up, along_y(up, 1)])
    right, left = along_x(stack, 1), along_x(stack, -1)
    return stack, right, left, along_x(right[:2], 1), along_x(left[2:], -1)


def scatter_ring(near, far):
    near = near + swap(far, "tgt", 1)
    piece = {dz: near[k] for k, dz in enumerate(RING)}
    up, down = along_z(piece[4], 1), along_z(piece[-3], -1)
    up, down = along_z(piece[3] + up, 1), along_z(piece[-2] + down, -1)
    up, down = along_z(piece[2] + up, 1), along_z(piece[-1] + down, -1)
    up = along_z(piece[1] + up, 1)
    return piece[0] + up + down


def scatter_quad(own, next_up, next_down, across_top, across_bottom, along):
    half = FEATS // 2
    top, bottom = along(across_top, 1), along(across_bottom, -1)
    up = jnp.concatenate([next_up[..., :half, :] + top, next_up[..., half:, :]], axis=-2)
    down = jnp.concatenate([next_down[..., :half, :], next_down[..., half:, :] + bottom], axis=-2)
    return own + along(up, 1) + along(down, -1)


def shards(
    src_feat, tgt_feat, row_pot, col_pot, src_mass, tgt_mass, rhs_src, rhs_tgt,
    tile_rows, tile_cols, tile_count,
):
    me_s, me_t = lax.axis_index("src"), lax.axis_index("tgt")
    meta = jnp.concatenate(
        [
            tile_rows.reshape(8),
            tile_cols.reshape(8),
            tile_count.reshape(1),
            me_s.reshape(1).astype(jnp.int32),
            me_t.reshape(1).astype(jnp.int32),
        ]
    )
    line = lambda v: v.reshape(1, PART)
    pay = (FEATS + 16, PART)
    pay_s, pay_t = pl.pallas_call(
        payload_kernel,
        out_shape=[shape(pay, BF16), shape(pay, BF16)],
        in_specs=[HBM] * 8,
        out_specs=[VMEM] * 2,
        scratch_shapes=[pltpu.VMEM((FEATS, PART), BF16)] * 2
        + [pltpu.VMEM((1, PART), F32)] * 6
        + [pltpu.SemaphoreType.DMA((8,))],
        compiler_params=params(24),
    )(
        src_feat, tgt_feat, line(row_pot), line(col_pot), line(src_mass), line(tgt_mass),
        line(rhs_src), line(rhs_tgt),
    )
    s_parts = gather_ring(pay_s)
    t_parts = gather_quad(pay_t)

    vec = shape((BLOCKS, TILE))
    two = shape((2 * BLOCKS, TILE))
    feats = shape((16, *pay), BF16)
    kern, xs, ys, bp, bq, dp, dq, rsum, csum = pl.pallas_call(
        build_kernel,
        out_shape=[
            pltpu.VMEM((SLOTS, TILE, TILE), F32), feats, feats, vec, vec, vec, vec, two, two,
        ],
        in_specs=[SMEM] + [ANY] * 7,
        out_specs=[VMEM] * 9,
        scratch_shapes=[
            pltpu.VMEM((TILE, 256), BF16),
            pltpu.VMEM((256, TILE), BF16),
            pltpu.VMEM((TILE, LANES), F32),
            pltpu.VMEM((TILE, LANES), F32),
            pltpu.VMEM((TILE, LANES), F32),
            pltpu.SemaphoreType.DMA((32,)),
        ],
        compiler_params=params(24),
    )(meta, *s_parts, *t_parts)
    kern = pltpu.with_memory_space_constraint(kern, pltpu.VMEM)

    row_pieces, col_pieces = sum_pieces(rsum, csum)
    v1p, v1q, gp, gq, rimg, cimg = pl.pallas_call(
        apply_kernel,
        out_shape=[vec, vec, vec, vec] + [shape((72, LANES))] * 2,
        in_specs=[SMEM] + [VMEM] * 9,
        out_specs=[VMEM] * 6,
        scratch_shapes=[pltpu.VMEM((TILE, LANES), F32)] * 2
        + [pltpu.VMEM((BLOCKS, TILE), F32)] * 2,
        compiler_params=params(24),
    )(meta, *row_pieces, *col_pieces, bp, bq, dp, dq, kern)

    row_pieces, col_pieces = sum_pieces(rimg, cimg)
    e1p, e1q, wp, wq, hp, hq, dots, known = pl.pallas_call(
        form_kernel,
        out_shape=[vec] * 6 + [shape((8, LANES))] * 2,
        in_specs=[SMEM] + [VMEM] * 11,
        out_specs=[VMEM] * 8,
        scratch_shapes=[pltpu.VMEM((TILE, LANES), F32), pltpu.VMEM((8, LANES), F32)],
        compiler_params=params(24),
    )(meta, *row_pieces, *col_pieces, bp, bq, v1p, v1q, gp, gq, kern)

    dots = doubled(dots, "tgt")
    dots = dots + swap(dots, "tgt", 8)
    dots = doubled(dots, "src")
    dots = (dots, swap(dots, "src", 8))
    outs = pl.pallas_call(
        grad_kernel,
        out_shape=[shape((1, PART))] * 2
        + [shape((8, FEATS, PART))] * 2
        + [shape((4, FEATS, PART))] * 3
        + [shape((4, FEATS // 2, PART))] * 2,
        in_specs=[SMEM] + [VMEM] * 14,
        out_specs=[VMEM] * 9,
        scratch_shapes=[
            pltpu.VMEM((BLOCKS, TILE), F32),
            pltpu.VMEM((BLOCKS, TILE), F32),
            pltpu.VMEM((TILE, LANES), F32),
            pltpu.VMEM((TILE, TILE), BF16),
            pltpu.VMEM((TILE, LANES), F32),
            pltpu.VMEM((BLOCKS, TILE), F32),
            pltpu.VMEM((BLOCKS, TILE), F32),
            pltpu.VMEM((BLOCKS, FEATS, TILE), F32),
            pltpu.VMEM((BLOCKS, FEATS, TILE), F32),
        ],
        compiler_params=params(24),
    )(meta, *dots, known, bp, bq, e1p, e1q, wp, wq, hp, hq, xs, ys, kern)
    adj_s, adj_t, near, far = outs[:4]
    grad_src = scatter_ring(near, far)
    part = scatter_quad(*outs[4:], along_x)
    half = FEATS // 2
    grad_tgt = scatter_quad(part[0], part[1], part[2], part[3, :half], part[3, half:], along_y)
    return adj_s.reshape(PART), adj_t.reshape(PART), grad_src, grad_tgt


def solution(mesh):
    in_specs = (
        P(None, ("src", "tgt")),
        P(None, ("tgt", "src")),
        P(("src", "tgt")),
        P(("tgt", "src")),
        P(("src", "tgt")),
        P(("tgt", "src")),
        P(("src", "tgt")),
        P(("tgt", "src")),
        P("src", "tgt", None),
        P("src", "tgt", None),
        P("src", "tgt"),
    )
    out_specs = (
        P(("src", "tgt")),
        P(("tgt", "src")),
        P(None, ("src", "tgt")),
        P(None, ("tgt", "src")),
    )
    return jax.shard_map(shards, mesh=mesh, in_specs=in_specs, out_specs=out_specs, check_vma=False)
```

time: 1640 us -> 272 us (0.17)
  blocking collectives: 1050 us -> 0 us
  waiting for transfers between devices: 302 us -> 95.6 us
  matrix products: 145 us -> 0 us
  starting transfers between devices: 0.24 us -> 131 us
  loops' own time: 44.1 us -> 0 us
  local copies, waits for them, and re-layouts: 50.6 us -> 9.77 us
  between operations: 30.2 us -> 2.06 us
  Pallas kernels: 0 us -> 20.9 us
    unnamed x6 -> x0, blocking collectives: 481 us -> none
    psum x5 -> x0, blocking collectives: 380 us -> none  [the longest x3 223 us: residual_squares(): return lax.psum(inner_local(vector, vector), ('src', 'tgt'))]
    unnamed x8 -> x0, waiting for transfers between devices: 272 us -> none
    all_gather x10 -> x0, blocking collectives: 189 us -> none  [the longest x4 83.9 us: spread_tgt(): return lax.all_gather(vector, 'src', axis=0, tiled=True)]
    dot_general x52 -> x0, matrix products: 145 us -> none  [the longest x12 53.9 us: update(): jnp.dot(kernel, tgt_piece, precision=lax.Precision.HIGHEST)]
    ppermute x0 -> x55, starting transfers between devices: none -> 131 us  [the longest x26 74.9 us: swap(): return lax.ppermute(value, axis, [(i, i ^ mask) for i in range(16)])]
    ppermute x0 -> x55, waiting for transfers between devices: none -> 95.6 us  [the longest x26 39.2 us: swap(): return lax.ppermute(value, axis, [(i, i ^ mask) for i in range(16)])]
    dynamic_slice x112 -> x0, local copies, waits for them, and re-layouts: 45.2 us -> none  [the longest x40 44.5 us: starts(): return (row_ids[slot_index] * TILE, col_ids[slot_index] * TILE)]
  transfers between devices with their start and end apart: 6 -> 55, of which waited for: 4 -> 35; matrix products, arithmetic and copies ran while one was open for 0% -> 2% of each run, Pallas kernels for 0% -> 0%
where the time goes in v1:
time: 272 us; the launch traced here: 267 us
  starting transfers between devices  131 us (48%)
  waiting for transfers between devices  95.6 us (35%)
  Pallas kernels  20.9 us (8%)
  local copies, waits for them, and re-layouts  9.77 us (4%)
  other arithmetic  7.15 us (3%)
    ppermute x26, starting transfers between devices, swap(): return lax.ppermute(value, axis, [(i, i ^ mask) for i in range(16)])  74.9 us
    ppermute x26, waiting for transfers between devices, swap(): return lax.ppermute(value, axis, [(i, i ^ mask) for i in range(16)])  39.2 us
    ppermute x8, waiting for transfers between devices, along_x(): lax.ppermute(value, 'src', [(i, i // 4 * 4 + (i + step) % 4) for i in ran...  32.7 us
    ppermute x8, starting transfers between devices, along_x(): lax.ppermute(value, 'src', [(i, i // 4 * 4 + (i + step) % 4) for i in ran...  28.4 us
    ppermute x14, waiting for transfers between devices, along_z(): lax.ppermute(value, 'tgt', [(i, (i + 2 * step) % 16) for i in range(16)])  23.7 us
    ppermute x14, starting transfers between devices, along_z(): lax.ppermute(value, 'tgt', [(i, (i + 2 * step) % 16) for i in range(16)])  19.1 us
    unnamed x67, local copies, waits for them, and re-layouts  9.12 us
    ppermute x7, starting transfers between devices, along_y(): lax.ppermute(value, 'src', [(i, (i + 4 * step) % 16) for i in range(16)])  8.9 us
  transfers between devices with their start and end apart: 55, of which 35 were waited for; matrix products, arithmetic and copies ran while one was open for 2% of the time, Pallas kernels for 0%

profile of v1, /device:TPU:24, one launch (start us, length us, event | category | flops | bytes accessed | tf_op | source)
XLA Modules:
  0.0 266.7 jit_solution(8180451415929223819)
XLA Ops:
  6.7 5.9 %collective-permute-start.1 = (bf16[80,512]{1,0:T(8,128)(2,1)S(1)}, bf16[80,512]{1,0:T(8,128)(2,1)S(1)}, u32[]{:S(2)}, u32[]{:S(2)}) collective-permute-start(bf16[80,512]{1,0:T(8,128)(2,1)S(1)} %get-tuple-element.38), channel_id=1, source_target_pairs={{0,14},{1,15},{2,0},{3,1},{4,2},{5,3},{6,4},{7,5},{8,6},{9,7},{10,... | collective-permute-start | bytes 245768 | tf_op jit(solution)/shard_map/ppermute | solution.py:455
  14.7 3.6 %collective-permute-start.3 = (bf16[80,512]{1,0:T(8,128)(2,1)S(1)}, bf16[80,512]{1,0:T(8,128)(2,1)S(1)}, u32[]{:S(2)}, u32[]{:S(2)}) collective-permute-start(bf16[80,512]{1,0:T(8,128)(2,1)S(1)} %collective-permute-done.1), channel_id=1, source_target_pairs={{0,14},{1,15},{2,0},{3,1},{4,2},{5,3},{6,4},{7,5},{8,6},{9,7},{10,... | collective-permute-start | bytes 245768 | tf_op jit(solution)/shard_map/ppermute | solution.py:455
  20.4 3.6 %collective-permute-start.5 = (bf16[80,512]{1,0:T(8,128)(2,1)S(1)}, bf16[80,512]{1,0:T(8,128)(2,1)S(1)}, u32[]{:S(2)}, u32[]{:S(2)}) collective-permute-start(bf16[80,512]{1,0:T(8,128)(2,1)S(1)} %collective-permute-done.3), channel_id=1, source_target_pairs={{0,14},{1,15},{2,0},{3,1},{4,2},{5,3},{6,4},{7,5},{8,6},{9,7},{10,... | collective-permute-start | bytes 245768 | tf_op jit(solution)/shard_map/ppermute | solution.py:455
  24.0 5.6 %collective-permute-done.4 = bf16[80,512]{1,0:T(8,128)(2,1)S(1)} collective-permute-done((bf16[80,512]{1,0:T(8,128)(2,1)S(1)}, bf16[80,512]{1,0:T(8,128)(2,1)S(1)}, u32[]{:S(2)}, u32[]{:S(2)}) %collective-permute-start.4) | collective-permute-done | bytes 81952 | tf_op jit(solution)/shard_map/ppermute | solution.py:455
  29.7 5.6 %collective-permute-done.6 = bf16[80,512]{1,0:T(8,128)(2,1)S(1)} collective-permute-done((bf16[80,512]{1,0:T(8,128)(2,1)S(1)}, bf16[80,512]{1,0:T(8,128)(2,1)S(1)}, u32[]{:S(2)}, u32[]{:S(2)}) %collective-permute-start.6) | collective-permute-done | bytes 81952 | tf_op jit(solution)/shard_map/ppermute | solution.py:455
  38.3 7.6 %collective-permute-done.12.t2 = bf16[4,80,512]{2,1,0:T(8,128)(2,1)S(1)} collective-permute-done((bf16[4,80,512]{2,1,0:T(8,128)(2,1)S(1)}, bf16[4,80,512]{2,1,0:T(8,128)(2,1)S(1)}, u32[]{:S(2)}, u32[]{:S(2)}) %collective-permute-start.12) | collective-permute-done | bytes 327712 | tf_op jit(solution)/shard_map/ppermute | solution.py:463
  45.9 3.8 %collective-permute-start.14 = (bf16[2,80,512]{2,1,0:T(8,128)(2,1)S(1)}, bf16[2,80,512]{2,1,0:T(8,128)(2,1)S(1)}, u32[]{:S(2)}, u32[]{:S(2)}) collective-permute-start(bf16[2,80,512]{2,1,0:T(8,128)(2,1)S(1)} %slice.107), channel_id=1, source_target_pairs={{0,48},{16,0},{32,16},{48,32},{64,112},{80,64},{96,80},{112,96},{1... | collective-permute-start | bytes 491528 | tf_op jit(solution)/shard_map/ppermute | solution.py:463
  58.0 7.8 %shard_map.139 = (f32[8,1024,1024]{2,1,0:T(8,128)S(1)}, bf16[16,80,512]{2,1,0:T(8,128)(2,1)}, bf16[16,80,512]{2,1,0:T(8,128)(2,1)}, f32[8,1024]{1,0:T(8,128)}, f...) custom-call(s32[19]{0:T(128)} %concatenate.15.meta, ...), custom_call_target="tpu_custom_call" | custom-call | tf_op jit(solution)/shard_map/pallas_call | solution.py:549
  65.8 19.7 %collective-permute-start.15 = (f32[16,1024]{1,0:T(8,128)}, f32[16,1024]{1,0:T(8,128)S(1)}, u32[]{:S(2)}, u32[]{:S(2)}) collective-permute-start(f32[16,1024]{1,0:T(8,128)} %get-tuple-element.40), channel_id=1, source_target_pairs={{0,1},{1,0},{2,3},{3,2},{4,5},{5,4},{6,7},{7,6},{8,9},{9,8},{10,11... | collective-permute-start | bytes 196616 | tf_op jit(solution)/shard_map/ppermute | solution.py:451
  92.8 3.9 %collective-permute-done.20 = f32[16,1024]{1,0:T(8,128)S(1)} collective-permute-done((f32[16,1024]{1,0:T(8,128)S(1)}, f32[16,1024]{1,0:T(8,128)S(1)}, u32[]{:S(2)}, u32[]{:S(2)}) %collective-permute-start.20) | collective-permute-done | bytes 65568 | tf_op jit(solution)/shard_map/ppermute | solution.py:451
  101.1 3.7 %collective-permute-start.22 = (f32[16,1024]{1,0:T(8,128)S(1)}, f32[16,1024]{1,0:T(8,128)S(1)}, u32[]{:S(2)}, u32[]{:S(2)}) collective-permute-start(f32[16,1024]{1,0:T(8,128)S(1)} %add.110.c0), channel_id=1, source_target_pairs={{0,128},{16,144},{32,160},{48,176},{64,192},{80,208},{96,224},{112... | collective-permute-start | bytes 196616 | tf_op jit(solution)/shard_map/ppermute | solution.py:451
  110.6 5.6 %collective-permute-start.23 = (f32[72,128]{1,0:T(8,128)}, f32[72,128]{1,0:T(8,128)S(1)}, u32[]{:S(2)}, u32[]{:S(2)}) collective-permute-start(f32[72,128]{1,0:T(8,128)} %get-tuple-element.47), channel_id=1, source_target_pairs={{0,1},{1,0},{2,3},{3,2},{4,5},{5,4},{6,7},{7,6},{8,9},{9,8},{10,11... | collective-permute-start | bytes 110600 | tf_op jit(solution)/shard_map/ppermute | solution.py:451
  133.0 4.0 %collective-permute-start.30 = (f32[72,128]{1,0:T(8,128)S(1)}, f32[72,128]{1,0:T(8,128)S(1)}, u32[]{:S(2)}, u32[]{:S(2)}) collective-permute-start(f32[72,128]{1,0:T(8,128)S(1)} %add.116.c0), channel_id=1, source_target_pairs={{0,128},{16,144},{32,160},{48,176},{64,192},{80,208},{96,224},{112... | collective-permute-start | bytes 110600 | tf_op jit(solution)/shard_map/ppermute | solution.py:451
  150.9 8.6 %collective-permute-start.33 = (f32[8,128]{1,0:T(8,128)S(1)}, f32[8,128]{1,0:T(8,128)S(1)}, u32[]{:S(2)}, u32[]{:S(2)}) collective-permute-start(f32[8,128]{1,0:T(8,128)S(1)} %add.118), channel_id=1, source_target_pairs={{0,4},{1,5},{2,6},{3,7},{4,0},{5,1},{6,2},{7,3},{8,12},{9,13},{10,... | collective-permute-start | bytes 12296 | tf_op jit(solution)/shard_map/ppermute | solution.py:451
  159.6 4.5 %collective-permute-done.33 = f32[8,128]{1,0:T(8,128)S(1)} collective-permute-done((f32[8,128]{1,0:T(8,128)S(1)}, f32[8,128]{1,0:T(8,128)S(1)}, u32[]{:S(2)}, u32[]{:S(2)}) %collective-permute-start.33) | collective-permute-done | bytes 4128 | tf_op jit(solution)/shard_map/ppermute | solution.py:451
  166.6 5.0 %collective-permute-done.34 = f32[8,128]{1,0:T(8,128)S(1)} collective-permute-done((f32[8,128]{1,0:T(8,128)S(1)}, f32[8,128]{1,0:T(8,128)S(1)}, u32[]{:S(2)}, u32[]{:S(2)}) %collective-permute-start.34) | collective-permute-done | bytes 4128 | tf_op jit(solution)/shard_map/ppermute | solution.py:451
  184.0 5.0 %collective-permute-start.38 = (f32[8,128]{1,0:T(8,128)S(1)}, f32[8,128]{1,0:T(8,128)S(1)}, u32[]{:S(2)}, u32[]{:S(2)}) collective-permute-start(f32[8,128]{1,0:T(8,128)S(1)} %add.123.q0), channel_id=1, source_target_pairs={{0,128},{16,144},{32,160},{48,176},{64,192},{80,208},{96,224},{112... | collective-permute-start | bytes 12296 | tf_op jit(solution)/shard_map/ppermute | solution.py:451
  191.2 7.3 %shard_map.142 = (f32[1,512]{1,0:T(1,128)}, f32[1,512]{1,0:T(1,128)}, f32[8,64,512]{2,1,0:T(8,128)}, f32[8,64,512]{2,1,0:T(8,128)}, f32[4,64,512]{2,1,0:T(8,128)...) custom-call(s32[19]{0:T(128)} %concatenate.15.meta, ...), custom_call_target="tpu_custom_call" | custom-call | tf_op jit(solution)/shard_map/pallas_call | solution.py:593
  198.5 18.0 %collective-permute-start.49 = (f32[4,32,512]{2,1,0:T(8,128)}, f32[4,32,512]{2,1,0:T(8,128)S(1)}, u32[]{:S(2)}, u32[]{:S(2)}) collective-permute-start(f32[4,32,512]{2,1,0:T(8,128)} %get-tuple-element.71), channel_id=1, source_target_pairs={{0,48},{16,0},{32,16},{48,32},{64,112},{80,64},{96,80},{112,96},{1... | collective-permute-start | bytes 786440 | tf_op jit(solution)/shard_map/ppermute | solution.py:463
  216.5 4.2 %collective-permute-done.49 = f32[4,32,512]{2,1,0:T(8,128)S(1)} collective-permute-done((f32[4,32,512]{2,1,0:T(8,128)}, f32[4,32,512]{2,1,0:T(8,128)S(1)}, u32[]{:S(2)}, u32[]{:S(2)}) %collective-permute-start.49) | collective-permute-done | bytes 262176 | tf_op jit(solution)/shard_map/ppermute | solution.py:463
  221.8 3.7 %collective-permute-start.50 = (f32[4,64,512]{2,1,0:T(8,128)S(1)}, f32[4,64,512]{2,1,0:T(8,128)S(1)}, u32[]{:S(2)}, u32[]{:S(2)}) collective-permute-start(f32[4,64,512]{2,1,0:T(8,128)S(1)} %pad_maximum_fusion.1), channel_id=1, source_target_pairs={{0,48},{16,0},{32,16},{48,32},{64,112},{80,64},{96,80},{112,96},{1... | collective-permute-start | bytes 1572872 | tf_op jit(solution)/shard_map/ppermute | solution.py:463
  227.2 5.3 %collective-permute-done.50 = f32[4,64,512]{2,1,0:T(8,128)S(1)} collective-permute-done((f32[4,64,512]{2,1,0:T(8,128)S(1)}, f32[4,64,512]{2,1,0:T(8,128)S(1)}, u32[]{:S(2)}, u32[]{:S(2)}) %collective-permute-start.50) | collective-permute-done | bytes 524320 | tf_op jit(solution)/shard_map/ppermute | solution.py:463
  232.5 9.1 %collective-permute-done.48 = f32[4,64,512]{2,1,0:T(8,128)S(1)} collective-permute-done((f32[4,64,512]{2,1,0:T(8,128)S(1)}, f32[4,64,512]{2,1,0:T(8,128)S(1)}, u32[]{:S(2)}, u32[]{:S(2)}) %collective-permute-start.48) | collective-permute-done | bytes 524320 | tf_op jit(solution)/shard_map/ppermute | solution.py:463
  249.9 4.4 %collective-permute-done.42 = f32[64,512]{1,0:T(8,128)S(1)} collective-permute-done((f32[64,512]{1,0:T(8,128)S(1)}, f32[64,512]{1,0:T(8,128)S(1)}, u32[]{:S(2)}, u32[]{:S(2)}) %collective-permute-start.42) | collective-permute-done | bytes 131104 | tf_op jit(solution)/shard_map/ppermute | solution.py:455
  (199 shorter events, 109.2 us)
Async XLA Ops:
  6.7 8.0 %collective-permute-start.1 = (bf16[80,512]{1,0:T(8,128)(2,1)S(1)}, bf16[80,512]{1,0:T(8,128)(2,1)S(1)}, u32[]{:S(2)}, u32[]{:S(2)}) collective-permute-start(bf16[80,512]{1,0:T(8,128)(2,1)S(1)} %get-tuple-element.38), channel_id=1, source_target_pairs={{0,14},{1,15},{2,0},{3,1},{4,2},{5,3},{6,4},{7,5},{8,6},{9,7},{10,... | collective-permute-start | bytes 245768 | tf_op jit(solution)/shard_map/ppermute | solution.py:455
  12.9 22.5 %collective-permute-start.8 = (bf16[80,512]{1,0:T(8,128)(2,1)S(1)}, bf16[80,512]{1,0:T(8,128)(2,1)S(1)}, u32[]{:S(2)}, u32[]{:S(2)}) collective-permute-start(bf16[80,512]{1,0:T(8,128)(2,1)S(1)} %get-tuple-element.39), channel_id=1, source_target_pairs={{0,192},{16,208},{32,224},{48,240},{64,0},{80,16},{96,32},{112,48}... | collective-permute-start | bytes 245768 | tf_op jit(solution)/shard_map/ppermute | solution.py:459
  18.3 17.1 %collective-permute-start.10 = (bf16[80,512]{1,0:T(8,128)(2,1)S(1)}, bf16[80,512]{1,0:T(8,128)(2,1)S(1)}, u32[]{:S(2)}, u32[]{:S(2)}) collective-permute-start(bf16[80,512]{1,0:T(8,128)(2,1)S(1)} %collective-permute-done.9), channel_id=1, source_target_pairs={{0,64},{16,80},{32,96},{48,112},{64,128},{80,144},{96,160},{112,17... | collective-permute-start | bytes 245768 | tf_op jit(solution)/shard_map/ppermute | solution.py:459
  20.4 9.3 %collective-permute-start.5 = (bf16[80,512]{1,0:T(8,128)(2,1)S(1)}, bf16[80,512]{1,0:T(8,128)(2,1)S(1)}, u32[]{:S(2)}, u32[]{:S(2)}) collective-permute-start(bf16[80,512]{1,0:T(8,128)(2,1)S(1)} %collective-permute-done.3), channel_id=1, source_target_pairs={{0,14},{1,15},{2,0},{3,1},{4,2},{5,3},{6,4},{7,5},{8,6},{9,7},{10,... | collective-permute-start | bytes 245768 | tf_op jit(solution)/shard_map/ppermute | solution.py:455
  35.3 21.3 %collective-permute-start.7 = (bf16[8,80,512]{2,1,0:T(8,128)(2,1)S(1)}, bf16[8,80,512]{2,1,0:T(8,128)(2,1)S(1)}, u32[]{:S(2)}, u32[]{:S(2)}) collective-permute-start(bf16[8,80,512]{2,1,0:T(8,128)(2,1)S(1)} %bitcast_dynamic-update-slice_fusion.s0), channel_id=1, source_target_pairs={{0,1},{1,0},{2,3},{3,2},{4,5},{5,4},{6,7},{7,6},{8,9},{9,8},{10,11... | collective-permute-start | bytes 1966088 | tf_op jit(solution)/shard_map/ppermute | solution.py:451
  35.5 10.4 %collective-permute-start.12 = (bf16[4,80,512]{2,1,0:T(8,128)(2,1)S(1)}, bf16[4,80,512]{2,1,0:T(8,128)(2,1)S(1)}, u32[]{:S(2)}, u32[]{:S(2)}) collective-permute-start(bf16[4,80,512]{2,1,0:T(8,128)(2,1)S(1)} %pad_maximum_fusion.2.t0), channel_id=1, source_target_pairs={{0,48},{16,0},{32,16},{48,32},{64,112},{80,64},{96,80},{112,96},{1... | collective-permute-start | bytes 983048 | tf_op jit(solution)/shard_map/ppermute | solution.py:463
  38.3 11.4 %collective-permute-start.11 = (bf16[4,80,512]{2,1,0:T(8,128)(2,1)S(1)}, bf16[4,80,512]{2,1,0:T(8,128)(2,1)S(1)}, u32[]{:S(2)}, u32[]{:S(2)}) collective-permute-start(bf16[4,80,512]{2,1,0:T(8,128)(2,1)S(1)} %pad_maximum_fusion.2.t0), channel_id=1, source_target_pairs={{0,16},{16,32},{32,48},{48,0},{64,80},{80,96},{96,112},{112,64},{1... | collective-permute-start | bytes 983048 | tf_op jit(solution)/shard_map/ppermute | solution.py:463
  45.9 7.1 %collective-permute-start.14 = (bf16[2,80,512]{2,1,0:T(8,128)(2,1)S(1)}, bf16[2,80,512]{2,1,0:T(8,128)(2,1)S(1)}, u32[]{:S(2)}, u32[]{:S(2)}) collective-permute-start(bf16[2,80,512]{2,1,0:T(8,128)(2,1)S(1)} %slice.107), channel_id=1, source_target_pairs={{0,48},{16,0},{32,16},{48,32},{64,112},{80,64},{96,80},{112,96},{1... | collective-permute-start | bytes 491528 | tf_op jit(solution)/shard_map/ppermute | solution.py:463
  49.7 6.8 %collective-permute-start.13 = (bf16[2,80,512]{2,1,0:T(8,128)(2,1)S(1)}, bf16[2,80,512]{2,1,0:T(8,128)(2,1)S(1)}, u32[]{:S(2)}, u32[]{:S(2)}) collective-permute-start(bf16[2,80,512]{2,1,0:T(8,128)(2,1)S(1)} %slice.106), channel_id=1, source_target_pairs={{0,16},{16,32},{32,48},{48,0},{64,80},{80,96},{96,112},{112,64},{1... | collective-permute-start | bytes 491528 | tf_op jit(solution)/shard_map/ppermute | solution.py:463
  65.8 20.8 %collective-permute-start.15 = (f32[16,1024]{1,0:T(8,128)}, f32[16,1024]{1,0:T(8,128)S(1)}, u32[]{:S(2)}, u32[]{:S(2)}) collective-permute-start(f32[16,1024]{1,0:T(8,128)} %get-tuple-element.40), channel_id=1, source_target_pairs={{0,1},{1,0},{2,3},{3,2},{4,5},{5,4},{6,7},{7,6},{8,9},{9,8},{10,11... | collective-permute-start | bytes 196616 | tf_op jit(solution)/shard_map/ppermute | solution.py:451
  98.3 8.3 %collective-permute-start.18 = (f32[16,1024]{1,0:T(8,128)S(1)}, f32[16,1024]{1,0:T(8,128)S(1)}, u32[]{:S(2)}, u32[]{:S(2)}) collective-permute-start(f32[16,1024]{1,0:T(8,128)S(1)} %add.107.r0), channel_id=1, source_target_pairs={{0,8},{1,9},{2,10},{3,11},{4,12},{5,13},{6,14},{7,15},{8,0},{9,1},... | collective-permute-start | bytes 196616 | tf_op jit(solution)/shard_map/ppermute | solution.py:451
  110.6 6.7 %collective-permute-start.23 = (f32[72,128]{1,0:T(8,128)}, f32[72,128]{1,0:T(8,128)S(1)}, u32[]{:S(2)}, u32[]{:S(2)}) collective-permute-start(f32[72,128]{1,0:T(8,128)} %get-tuple-element.47), channel_id=1, source_target_pairs={{0,1},{1,0},{2,3},{3,2},{4,5},{5,4},{6,7},{7,6},{8,9},{9,8},{10,11... | collective-permute-start | bytes 110600 | tf_op jit(solution)/shard_map/ppermute | solution.py:451
  118.1 7.4 %collective-permute-start.24 = (f32[72,128]{1,0:T(8,128)S(1)}, f32[72,128]{1,0:T(8,128)S(1)}, u32[]{:S(2)}, u32[]{:S(2)}) collective-permute-start(f32[72,128]{1,0:T(8,128)S(1)} %add.111), channel_id=1, source_target_pairs={{0,2},{1,3},{2,0},{3,1},{4,6},{5,7},{6,4},{7,5},{8,10},{9,11},{10,... | collective-permute-start | bytes 110600 | tf_op jit(solution)/shard_map/ppermute | solution.py:451
  130.9 8.3 %collective-permute-start.26 = (f32[72,128]{1,0:T(8,128)S(1)}, f32[72,128]{1,0:T(8,128)S(1)}, u32[]{:S(2)}, u32[]{:S(2)}) collective-permute-start(f32[72,128]{1,0:T(8,128)S(1)} %add.113.r0), channel_id=1, source_target_pairs={{0,8},{1,9},{2,10},{3,11},{4,12},{5,13},{6,14},{7,15},{8,0},{9,1},... | collective-permute-start | bytes 110600 | tf_op jit(solution)/shard_map/ppermute | solution.py:451
  150.9 13.1 %collective-permute-start.33 = (f32[8,128]{1,0:T(8,128)S(1)}, f32[8,128]{1,0:T(8,128)S(1)}, u32[]{:S(2)}, u32[]{:S(2)}) collective-permute-start(f32[8,128]{1,0:T(8,128)S(1)} %add.118), channel_id=1, source_target_pairs={{0,4},{1,5},{2,6},{3,7},{4,0},{5,1},{6,2},{7,3},{8,12},{9,13},{10,... | collective-permute-start | bytes 12296 | tf_op jit(solution)/shard_map/ppermute | solution.py:451
  164.1 7.5 %collective-permute-start.34 = (f32[8,128]{1,0:T(8,128)S(1)}, f32[8,128]{1,0:T(8,128)S(1)}, u32[]{:S(2)}, u32[]{:S(2)}) collective-permute-start(f32[8,128]{1,0:T(8,128)S(1)} %add.119), channel_id=1, source_target_pairs={{0,8},{1,9},{2,10},{3,11},{4,12},{5,13},{6,14},{7,15},{8,0},{9,1},... | collective-permute-start | bytes 12296 | tf_op jit(solution)/shard_map/ppermute | solution.py:451
  198.5 22.2 %collective-permute-start.49 = (f32[4,32,512]{2,1,0:T(8,128)}, f32[4,32,512]{2,1,0:T(8,128)S(1)}, u32[]{:S(2)}, u32[]{:S(2)}) collective-permute-start(f32[4,32,512]{2,1,0:T(8,128)} %get-tuple-element.71), channel_id=1, source_target_pairs={{0,48},{16,0},{32,16},{48,32},{64,112},{80,64},{96,80},{112,96},{1... | collective-permute-start | bytes 786440 | tf_op jit(solution)/shard_map/ppermute | solution.py:463
  216.4 10.4 %collective-permute-start.39 = (f32[8,64,512]{2,1,0:T(8,128)}, f32[8,64,512]{2,1,0:T(8,128)S(1)}, u32[]{:S(2)}, u32[]{:S(2)}) collective-permute-start(f32[8,64,512]{2,1,0:T(8,128)} %get-tuple-element.66), channel_id=1, source_target_pairs={{0,1},{1,0},{2,3},{3,2},{4,5},{5,4},{6,7},{7,6},{8,9},{9,8},{10,11... | collective-permute-start | bytes 3145736 | tf_op jit(solution)/shard_map/ppermute | solution.py:451
  216.5 10.1 %collective-permute-start.47 = (f32[4,32,512]{2,1,0:T(8,128)}, f32[4,32,512]{2,1,0:T(8,128)S(1)}, u32[]{:S(2)}, u32[]{:S(2)}) collective-permute-start(f32[4,32,512]{2,1,0:T(8,128)} %get-tuple-element.69), channel_id=1, source_target_pairs={{0,16},{16,32},{32,48},{48,0},{64,80},{80,96},{96,112},{112,64},{1... | collective-permute-start | bytes 786440 | tf_op jit(solution)/shard_map/ppermute | solution.py:463
  221.8 10.7 %collective-permute-start.50 = (f32[4,64,512]{2,1,0:T(8,128)S(1)}, f32[4,64,512]{2,1,0:T(8,128)S(1)}, u32[]{:S(2)}, u32[]{:S(2)}) collective-permute-start(f32[4,64,512]{2,1,0:T(8,128)S(1)} %pad_maximum_fusion.1), channel_id=1, source_target_pairs={{0,48},{16,0},{32,16},{48,32},{64,112},{80,64},{96,80},{112,96},{1... | collective-permute-start | bytes 1572872 | tf_op jit(solution)/shard_map/ppermute | solution.py:463
  226.7 14.8 %collective-permute-start.48 = (f32[4,64,512]{2,1,0:T(8,128)S(1)}, f32[4,64,512]{2,1,0:T(8,128)S(1)}, u32[]{:S(2)}, u32[]{:S(2)}) collective-permute-start(f32[4,64,512]{2,1,0:T(8,128)S(1)} %pad_maximum_fusion), channel_id=1, source_target_pairs={{0,16},{16,32},{32,48},{48,0},{64,80},{80,96},{96,112},{112,64},{1... | collective-permute-start | bytes 1572872 | tf_op jit(solution)/shard_map/ppermute | solution.py:463
  227.1 14.6 %collective-permute-start.40 = (f32[64,512]{1,0:T(8,128)S(1)}, f32[64,512]{1,0:T(8,128)S(1)}, u32[]{:S(2)}, u32[]{:S(2)}) collective-permute-start(f32[64,512]{1,0:T(8,128)S(1)} %get-tuple-element.74), channel_id=1, source_target_pairs={{0,2},{1,3},{2,4},{3,5},{4,6},{5,7},{6,8},{7,9},{8,10},{9,11},{10,... | collective-permute-start | bytes 393224 | tf_op jit(solution)/shard_map/ppermute | solution.py:455
  254.4 6.7 %collective-permute-start.54 = (f32[64,512]{1,0:T(8,128)S(1)}, f32[64,512]{1,0:T(8,128)S(1)}, u32[]{:S(2)}, u32[]{:S(2)}) collective-permute-start(f32[64,512]{1,0:T(8,128)S(1)} %pad_maximum_fusion.4), channel_id=1, source_target_pairs={{0,192},{16,208},{32,224},{48,240},{64,0},{80,16},{96,32},{112,48}... | collective-permute-start | bytes 393224 | tf_op jit(solution)/shard_map/ppermute | solution.py:459
  254.5 6.6 %collective-permute-start.52 = (f32[64,512]{1,0:T(8,128)S(1)}, f32[64,512]{1,0:T(8,128)S(1)}, u32[]{:S(2)}, u32[]{:S(2)}) collective-permute-start(f32[64,512]{1,0:T(8,128)S(1)} %pad_maximum_fusion.3), channel_id=1, source_target_pairs={{0,64},{16,80},{32,96},{48,112},{64,128},{80,144},{96,160},{112,17... | collective-permute-start | bytes 393224 | tf_op jit(solution)/shard_map/ppermute | solution.py:459
  (61 other events, 401.2 us)

commit v2 on v1

v2 whole, which is shorter than its diff:
```python
import math

import jax
import jax.numpy as jnp
from jax import lax
from jax.experimental import pallas as pl
from jax.experimental.pallas import tpu as pltpu
from jax.sharding import PartitionSpec as P

TILE = 1024
FEATS = 64
LANES = 128
BLOCKS = 8
SLOTS = 8
PART = 512
EPS = 0.05
RHO = 1.0
SCALE = 2.0 * math.log2(math.e) / EPS
DOWN = 2.0**-40
UP = 2.0**40
F32 = jnp.float32
BF16 = jnp.bfloat16
VMEM = pl.BlockSpec(memory_space=pltpu.VMEM)
SMEM = pl.BlockSpec(memory_space=pltpu.SMEM)
ANY = pl.BlockSpec(memory_space=pl.ANY)
HBM = pl.BlockSpec(memory_space=pltpu.HBM)
RING = (0, -1, 1, 4, -2, -3, 2, 3)
QUAD = (0, 1, -1, 2)


def params(mib):
    return pltpu.CompilerParams(vmem_limit_bytes=mib * 2**20)


def shape(dims, dtype=F32):
    return jax.ShapeDtypeStruct(dims, dtype)


def split3(value):
    high = value.astype(BF16).astype(F32)
    rest = value - high
    middle = rest.astype(BF16).astype(F32)
    low = (rest - middle).astype(BF16).astype(F32)
    return high, middle, low


def to_positions(value, turned):
    turned[...] = value.T
    groups = [turned[pl.ds(g, 8, stride=64), :] for g in range(64)]
    return jnp.concatenate(groups, axis=0).T


def to_cells(value, turned):
    turned[...] = value.T
    groups = [turned[pl.ds(r, 64, stride=8), :] for r in range(8)]
    return jnp.concatenate(groups, axis=0).T


def payload_kernel(*refs):
    sources, (out_s, out_t), held = refs[:8], refs[8:10], refs[10:18]
    turned, sems = refs[18:]
    copies = [
        pltpu.make_async_copy(source, place, sems.at[i])
        for i, (source, place) in enumerate(zip(sources, held))
    ]
    for copy in copies:
        copy.start()
    for copy in copies:
        copy.wait()
    sf, tf, rp, cp, sm, tm, rs, rt = held
    for feat, pot, mass, rhs, out, first in (
        (sf, rp, sm, rs, out_s, True),
        (tf, cp, tm, rt, out_t, False),
    ):
        wide = feat[...].astype(F32)
        potential = pot[...]
        term = (potential - jnp.sum(wide * wide, axis=0, keepdims=True)) * 0.5
        damp = EPS / RHO * mass[...] * jnp.exp(-potential / RHO)
        ones = jnp.ones((3, PART), F32)
        pieces = list(split3(term))
        rows = pieces + [ones] if first else [ones] + pieces
        rows += list(split3(rhs[...])) + list(split3(damp))
        rows.append(jnp.zeros((4, PART), F32))
        tail = jnp.concatenate(rows, axis=0)
        if first:
            whole = jnp.concatenate([wide, tail, jnp.zeros((48, PART), F32)], axis=0)
            whole = to_positions(whole, turned)
            out[0:FEATS, :] = whole[:FEATS].astype(BF16)
            keep = lax.broadcasted_iota(jnp.int32, (16, PART), 0) < 6
            tail = jnp.where(keep, whole[FEATS : FEATS + 16], tail)
        else:
            out[0:FEATS, :] = feat[...]
        out[FEATS : FEATS + 16, :] = tail.astype(BF16)


def three(rows, start):
    return rows[start : start + 1] + (rows[start + 1 : start + 2] + rows[start + 2 : start + 3])


def lane_blocks(row, height):
    return [
        jnp.broadcast_to(row[:, LANES * l : LANES * (l + 1)], (height, LANES))
        for l in range(TILE // LANES)
    ]


def total(values):
    result = values[0]
    for value in values[1:]:
        result = result + value
    return result


def block_rows(block):
    return pl.ds(pl.multiple_of(8 * block, 8), 8)


def fill_columns(column, packed):
    for g in range(LANES):
        column[8 * g : 8 * g + 8, :] = jnp.broadcast_to(packed[:, g : g + 1], (8, LANES))


def lane_sums(partial):
    lane = lax.broadcasted_iota(jnp.int32, (8, LANES), 1)
    result = jnp.zeros((8, LANES), F32)
    for g in range(LANES):
        group = jnp.sum(partial[8 * g : 8 * g + 8, :], axis=1, keepdims=True)
        result = jnp.where(lane == g, group, result)
    return result


def add_block(ref, first, block, value):
    rows = pl.ds(pl.multiple_of(first + 8 * block, 8), 8)
    ref[rows, :] = ref[rows, :] + value


def add_sums(ref, index, sums):
    row = jnp.sum(jnp.concatenate(sums, axis=1), axis=0, keepdims=True)
    ref[pl.ds(index, 1), :] = ref[pl.ds(index, 1), :] + row


def unpack(value):
    return jnp.concatenate(
        [value[BLOCKS * l : BLOCKS * (l + 1)] for l in range(TILE // LANES)], axis=1
    )


def pack_into(out, first, value):
    for l in range(TILE // LANES):
        out[first + BLOCKS * l : first + BLOCKS * (l + 1), :] = value[:, LANES * l : LANES * (l + 1)]


def pair_of(ref, block):
    return jnp.concatenate([ref[2 * block], ref[2 * block + 1]], axis=1)


def ring_block(me, dz, other):
    place = lax.rem(me // 2 + (dz + 8), 8)
    core = lax.rem(me, 2)
    return 2 * place + (1 - core if other else core)


def quad_block(me, dy, dx):
    return 4 * lax.rem(me // 4 + (dy + 4), 4) + lax.rem(lax.rem(me, 4) + (dx + 4), 4)


def fetch(kern, held, sems, slot):
    place = lax.rem(slot, 3)
    return pltpu.make_async_copy(kern.at[slot], held.at[place], sems.at[place])


def start_fetching(kern, held, sems, count):
    fetch(kern, held, sems, 0).start()

    @pl.when(count > 1)
    def _():
        fetch(kern, held, sems, 1).start()


def next_tile(kern, held, sems, slot, count):
    @pl.when(slot + 2 < count)
    def _():
        fetch(kern, held, sems, slot + 2).start()

    fetch(kern, held, sems, slot).wait()
    return held.at[lax.rem(slot, 3)]


WIDE = TILE // LANES


def no_sums():
    return tuple(jnp.zeros((8, LANES), F32) for l in range(WIDE))


def lanes_of(l):
    return slice(LANES * l, LANES * (l + 1))


def build_kernel(
    meta, s0, s1, t0, t1, t2, t3, t4,
    kern, stored, xs, ys, pb, qb, rout, cout,
    left, right, sums, prods, column, csum, parts, sems, out_sems,
):
    me_s, me_t = meta[17], meta[18]
    copies = []
    for k in range(8):
        for other, stack in enumerate((s0, s1)):
            copies.append((stack.at[k], xs.at[ring_block(me_t, RING[k], other)]))
    for k in range(4):
        far = (t3.at[k] if k < 2 else t4.at[k - 2])
        for dx, piece in ((0, t0.at[k]), (1, t2.at[k]), (-1, t1.at[k]), (2, far)):
            copies.append((piece, ys.at[quad_block(me_s, QUAD[k], dx)]))
    copies = [
        pltpu.make_async_copy(source, place, sems.at[i])
        for i, (source, place) in enumerate(copies)
    ]
    for copy in copies:
        copy.start()
    rout[...] = jnp.zeros_like(rout)
    csum[...] = jnp.zeros_like(csum)
    for copy in copies:
        copy.wait()
    for part in range(16):
        for place, ref in ((0, xs), (2, ys)):
            rows = ref[part, FEATS : FEATS + 16, :].astype(F32)
            at = part // 2 + 8 * (part % 2)
            parts[place, at : at + 1, :] = three(rows, 6)
            parts[place + 1, at : at + 1, :] = three(rows, 9)
    for place in range(2):
        even, odd = parts[place, 0:8, :], parts[place, 8:16, :]
        for r in range(8):
            cells = slice(64 * r, 64 * (r + 1))
            pb[pl.ds(64 * place + r, 8, stride=8), :] = jnp.concatenate(
                [even[:, cells], odd[:, cells]], axis=1
            )
        for side in range(2):
            qb[8 * place : 8 * place + 8, PART * side : PART * (side + 1)] = parts[
                2 + place, 8 * side : 8 * side + 8, :
            ]

    def store(slot):
        return pltpu.make_async_copy(kern.at[slot], stored.at[slot], out_sems.at[slot])

    keep = lax.broadcasted_iota(jnp.int32, (16, TILE), 0) < 6
    blank = jnp.zeros((48, TILE), BF16)

    def with_terms(payload):
        terms = jnp.where(keep, payload[FEATS:].astype(F32), 0.0).astype(BF16)
        return jnp.concatenate([payload[:FEATS], terms, blank], axis=0)

    def tile(slot, carry):
        rb, cb = meta[slot], meta[8 + slot]
        kernel = kern.at[slot]
        left[...] = with_terms(pair_of(xs, rb)).T
        right[...] = with_terms(pair_of(ys, cb))
        for strip in range(4):
            cells = slice(256 * strip, 256 * (strip + 1))
            kernel[:, cells] = jnp.dot(left[...], right[:, cells], preferred_element_type=F32)
        q = lane_blocks(qb[pl.ds(cb, 1), :], 8)
        fill_columns(column, pb[block_rows(rb), :])

        def rows_of(step, accs):
            csums, cprods = accs
            for u in range(4):
                at = pl.ds(pl.multiple_of(step * 32 + 8 * u, 8), 8)
                ks = [jnp.exp2(kernel[at, lanes_of(l)] * SCALE) for l in range(WIDE)]
                for l in range(WIDE):
                    kernel[at, lanes_of(l)] = ks[l]
                p = column[at, :]
                sums[at, :] = total(ks)
                prods[at, :] = total([ks[l] * q[l] for l in range(WIDE)])
                csums = tuple(csums[l] + ks[l] for l in range(WIDE))
                cprods = tuple(cprods[l] + ks[l] * p for l in range(WIDE))
            return csums, cprods

        csums, cprods = lax.fori_loop(0, TILE // 32, rows_of, (no_sums(), no_sums()))
        store(slot).start()
        add_block(rout, 0, rb, lane_sums(sums))
        add_block(rout, 64, rb, lane_sums(prods))
        add_sums(csum, cb, csums)
        add_sums(csum, 8 + cb, cprods)
        return carry

    count = meta[16]
    lax.fori_loop(0, count, tile, 0)
    pack_into(cout, 0, csum[:8, :])
    pack_into(cout, 64, csum[8:, :])

    def finish(slot, carry):
        store(slot).wait()
        return carry

    lax.fori_loop(0, count, finish, 0)


def folded(value, join):
    if value.shape[1] == LANES:
        return value
    result = value[:, :LANES]
    for l in range(1, WIDE):
        result = join(result, value[:, lanes_of(l)])
    return result


def lane_partial(value):
    return folded(jnp.sum(value, axis=0, keepdims=True), jnp.add)


def lane_largest(value):
    return folded(jnp.max(value, axis=0, keepdims=True), jnp.maximum)


def scalar(row):
    return jnp.sum(row, axis=1, keepdims=True)


def apply_kernel(
    meta, rows_in, cols_in, pb, qb, kern,
    pv, qv, rout, cout,
    prods, column, csum,
):
    rows = (rows_in[:64, :], rows_in[64:, :])
    cols = (unpack(cols_in[:64, :]), unpack(cols_in[64:, :]))
    rout[...] = jnp.zeros_like(rout)
    csum[...] = jnp.zeros_like(csum)
    cout[64:128, :] = jnp.zeros((64, LANES), F32)
    for (marg, prod), given, out, image, height in (
        (rows, pb, pv, cout, 64),
        (cols, qb, qv, rout, 8),
    ):
        b, d = given[:height, :], given[height:, :]
        g = marg + d
        v = g * (b * DOWN) + prod * DOWN
        out[:height, :] = v
        out[height:, :] = g
        for place, value in enumerate(
            (lane_partial(b * b), lane_partial(b * v), lane_partial(v * v), lane_largest(g))
        ):
            image[64 + place : 65 + place, :] = value

    def tile(slot, carry):
        rb, cb = meta[slot], meta[8 + slot]
        kernel = kern.at[slot]
        q = lane_blocks(qv[pl.ds(cb, 1), :], 8)
        fill_columns(column, pv[block_rows(rb), :])

        def rows_of(step, cprods):
            for u in range(4):
                at = pl.ds(pl.multiple_of(step * 32 + 8 * u, 8), 8)
                ks = [kernel[at, lanes_of(l)] for l in range(WIDE)]
                p = column[at, :]
                prods[at, :] = total([ks[l] * q[l] for l in range(WIDE)])
                cprods = tuple(cprods[l] + ks[l] * p for l in range(WIDE))
            return cprods

        cprods = lax.fori_loop(0, TILE // 32, rows_of, no_sums())
        add_block(rout, 0, rb, lane_sums(prods))
        add_sums(csum, cb, cprods)
        return carry

    lax.fori_loop(0, meta[16], tile, 0)
    pack_into(cout, 0, csum[...])


def form_kernel(
    meta, rows_in, cols_in, pb, qb, pv, qv, kern,
    pw, qw, dots, known,
    column, acc,
):
    both = rows_in[64:72, :] + cols_in[64:72, :]
    bb, bv, vv, sigma = (scalar(both[i : i + 1]) for i in range(4))
    rows, cols = rows_in[:64, :], unpack(cols_in[:64, :])
    inverse = 1.0 / sigma
    lift = UP * inverse
    alpha = bb / (bv * lift)
    known[...] = jnp.zeros_like(known)
    for place, value in enumerate((bb, bv * lift, (vv * lift) * lift, inverse)):
        known[place : place + 1, :] = jnp.broadcast_to(value, (1, LANES))
    found = []
    for given, vectors, image, out, height in ((pb, pv, rows, pw, 64), (qb, qv, cols, qw, 8)):
        b, v, g = given[:height, :], vectors[:height, :], vectors[height:, :]
        second = g * v + image
        first = v * lift
        next_image = (second * lift) * inverse
        residual = b - alpha * first
        turned = first - alpha * next_image
        out[:height, :] = residual
        out[height : 2 * height, :] = turned
        out[2 * height :, :] = first
        found.append(
            (
                lane_partial(residual * residual),
                lane_partial(residual * turned),
                lane_partial(residual * first),
                lane_partial(turned * turned),
                lane_partial(turned * first),
                lane_partial(next_image * turned),
                lane_partial(first * next_image),
                lane_partial((g * inverse) * turned * turned),
            )
        )
    acc[...] = jnp.zeros_like(acc)

    def tile(slot, carry):
        rb, cb = meta[slot], meta[8 + slot]
        kernel = kern.at[slot]
        q = lane_blocks(qw[pl.ds(8 + cb, 1), :] * inverse, 8)
        fill_columns(column, pw[pl.ds(pl.multiple_of(64 + 8 * rb, 8), 8), :])

        def rows_of(step, cprods):
            for u in range(4):
                at = pl.ds(pl.multiple_of(step * 32 + 8 * u, 8), 8)
                p = column[at, :]
                cprods = tuple(cprods[l] + kernel[at, lanes_of(l)] * p for l in range(WIDE))
            return cprods

        cprods = lax.fori_loop(0, TILE // 32, rows_of, no_sums())
        acc[...] = acc[...] + total([cprods[l] * q[l] for l in range(WIDE)])
        return carry

    lax.fori_loop(0, meta[16], tile, 0)
    for place in range(8):
        value = (found[0][place] + found[1][place]) * (1.0 / 16.0)
        if place == 7:
            value = value + 2.0 * jnp.sum(acc[...], axis=0, keepdims=True)
        dots[place : place + 1, :] = value


def grad_kernel(
    meta, dots, known, pb, qb, pw, qw, xs, ys, kern,
    adj_s, adj_t, near, far, x0, x1, x2, x3, x4,
    ap, aq, column, half, row_wy, col_wx, held, sems,
):
    tiles = meta[16]
    start_fetching(kern, held, sems, tiles)
    me_s, me_t = meta[17], meta[18]
    ee, ew, eh, ww, wh, uw, hu, waw = (scalar(dots[i : i + 1, :]) for i in range(8))
    bb, bh, hh, inverse = (known[i : i + 1, 0:1] for i in range(4))
    alpha1 = bb / bh
    beta1 = ee / bb
    dad = ew + 2.0 * beta1 * eh + beta1 * beta1 * bh
    alpha2 = ee / dad
    e_ad = ew + beta1 * eh
    ad_ad = ww + 2.0 * beta1 * wh + beta1 * beta1 * hh
    rr2 = ee - 2.0 * alpha2 * e_ad + alpha2 * alpha2 * ad_ad
    beta2 = rr2 / ee
    form = waw + 2.0 * beta1 * uw + beta1 * beta1 * hu
    r_ar = ew - 2.0 * alpha2 * (ww + beta1 * wh) + alpha2 * alpha2 * form
    d2_ar2 = ew + beta1 * eh - alpha2 * ad_ad
    d3ad3 = r_ar + 2.0 * beta2 * d2_ar2 + beta2 * beta2 * dad
    alpha3 = rr2 / d3ad3
    on_b = (alpha1 + alpha2 * beta1 + alpha3 * beta2 * beta1) * inverse
    on_e = (alpha2 + alpha3 * (1.0 + beta2)) * inverse
    on_w = -(alpha3 * alpha2) * inverse
    on_h = on_w * beta1
    for given, vectors, out, height in ((pb, pw, ap, 64), (qb, qw, aq, 8)):
        e, w, h = (vectors[height * i : height * (i + 1), :] for i in range(3))
        out[...] = on_b * given[:height, :] + on_e * e + on_w * w + on_h * h
    own = ap[block_rows(me_t // 2), :]
    own = jnp.where(me_t % 2 == 1, own[:, 64:], own[:, :64])
    for r in range(8):
        adj_s[:, 64 * r : 64 * (r + 1)] = own[r : r + 1, :]
    row = aq[pl.ds(me_s // 2, 1), :]
    adj_t[...] = jnp.where(me_s % 2 == 1, row[:, PART:], row[:, :PART])
    row_wy[...] = jnp.zeros_like(row_wy)
    col_wx[...] = jnp.zeros_like(col_wx)

    def tile(slot, carry):
        rb, cb = meta[slot], meta[8 + slot]
        fill_columns(column, ap[block_rows(rb), :])
        q = lane_blocks(aq[pl.ds(cb, 1), :], 16)
        kernel = next_tile(kern, held, sems, slot, tiles)

        def rows_of(step, unused):
            for u in range(2):
                at = pl.ds(pl.multiple_of(step * 32 + 16 * u, 16), 16)
                p = column[at, :]
                for l in range(WIDE):
                    half[at, lanes_of(l)] = (kernel[at, lanes_of(l)] * (p + q[l])).astype(BF16)
            return unused

        lax.fori_loop(0, TILE // 32, rows_of, 0)
        row_wy[rb] = row_wy[rb] + lax.dot_general(
            pair_of(ys, cb), half[...], (((1,), (1,)), ((), ())), preferred_element_type=F32
        )
        col_wx[cb] = col_wx[cb] + jnp.dot(
            pair_of(xs, rb), half[...], preferred_element_type=F32
        )
        return carry

    lax.fori_loop(0, tiles, tile, 0)


    def part_of(feat, mixed, ones, block):
        wide = feat[block, :FEATS, :].astype(F32)
        odd = block % 2 == 1
        whole = mixed[block // 2]
        mine = jnp.where(odd, whole[:, PART:], whole[:, :PART])
        return (2.0 / EPS) * (wide * mine[ones : ones + 1] - mine[:FEATS])

    for k in range(8):
        for other, out in enumerate((near, far)):
            out[k] = part_of(xs, row_wy, FEATS, ring_block(me_t, RING[k], other))
    for k in range(4):
        for dx, out in ((0, x0), (1, x1), (-1, x2), (2, None)):
            part = part_of(ys, col_wx, FEATS + 3, quad_block(me_s, QUAD[k], dx))
            if out is None:
                x3[k] = part[:32]
                x4[k] = part[32:]
            else:
                out[k] = part


def finish_kernel(p0, p1, p2, p3, p4, p5, out, turned):
    value = ((p0[...] + p1[...]) + p2[...]) + ((p3[...] + p4[...]) + p5[...])
    value = jnp.concatenate([value, jnp.zeros_like(value)], axis=0)
    out[...] = to_cells(value, turned)[:FEATS]


def swap(value, axis, mask):
    return lax.ppermute(value, axis, [(i, i ^ mask) for i in range(16)])


def along_z(value, step):
    return lax.ppermute(value, "tgt", [(i, (i + 2 * step) % 16) for i in range(16)])


def along_y(value, step):
    return lax.ppermute(value, "src", [(i, (i + 4 * step) % 16) for i in range(16)])


def along_x(value, step):
    return lax.ppermute(value, "src", [(i, i // 4 * 4 + (i + step) % 4) for i in range(16)])


def exchange(value, axis):
    return lax.all_to_all(value, axis, 0, 0)


def summed(value, axis):
    everywhere = jnp.broadcast_to(value[None], (16, *value.shape))
    return jnp.sum(exchange(everywhere, axis), axis=0)


def sum_pieces(row, col):
    for mask in (1, 2, 4, 8):
        row, col = together(row + swap(row, "tgt", mask), col + swap(col, "src", mask))
    return row, col


def together(*values):
    return lax.optimization_barrier(values)


def gather_all(own_s, own_t):
    after, before, across = along_z(own_s, 1), along_z(own_s, -1), along_z(own_s, 4)
    up, down, over = along_y(own_t, 1), along_y(own_t, -1), along_y(own_t, 2)
    after, before, across, up, down, over = together(after, before, across, up, down, over)
    stack = jnp.stack([own_t, down, up, over])
    low, high = jnp.stack([own_s, after]), jnp.stack([own_s, before])
    right, left = along_x(stack, 1), along_x(stack, -1)
    low, high = along_z(low, 2), along_z(high, -2)
    right, left, low, high = together(right, left, low, high)
    near = jnp.concatenate([jnp.stack([own_s, after, before, across]), low, high])
    far = swap(near, "tgt", 1)
    return (near, far), (stack, right, left, along_x(right[:2], 1), along_x(left[2:], -1))


def scatter_all(near, far, own, next_up, next_down, top, bottom):
    half = FEATS // 2
    other = swap(far, "tgt", 1)
    top, bottom = along_x(top, 1), along_x(bottom, -1)
    other, top, bottom = together(other, top, bottom)
    near = near + other
    up = jnp.concatenate([next_up[:, :half] + top, next_up[:, half:]], axis=1)
    down = jnp.concatenate([next_down[:, :half], next_down[:, half:] + bottom], axis=1)
    up, down = along_x(up, 1), along_x(down, -1)
    after, before = along_z(near[6:8], 2), along_z(near[4:6], -2)
    up, down, after, before = together(up, down, after, before)
    part = (own + up) + down
    last = (
        along_z(near[2] + after[1], 1),
        along_z(near[1] + before[1], -1),
        along_z(near[3], 4),
        along_y(part[1], 1),
        along_y(part[2], -1),
        along_y(part[3], 2),
    )
    last = together(*last)
    grad_src = pl.pallas_call(
        finish_kernel,
        out_shape=shape((FEATS, PART)),
        in_specs=[VMEM] * 6,
        out_specs=VMEM,
        scratch_shapes=[pltpu.VMEM((PART, LANES), F32)],
        compiler_params=params(24),
    )(near[0], after[0], before[0], *last[:3])
    grad_tgt = (part[0] + last[3]) + (last[4] + last[5])
    return grad_src, grad_tgt


def shards(
    src_feat, tgt_feat, row_pot, col_pot, src_mass, tgt_mass, rhs_src, rhs_tgt,
    tile_rows, tile_cols, tile_count,
):
    me_s, me_t = lax.axis_index("src"), lax.axis_index("tgt")
    meta = jnp.concatenate(
        [
            tile_rows.reshape(8),
            tile_cols.reshape(8),
            tile_count.reshape(1),
            me_s.reshape(1).astype(jnp.int32),
            me_t.reshape(1).astype(jnp.int32),
        ]
    )
    line = lambda v: v.reshape(1, PART)
    pay = (FEATS + 16, PART)
    pay_s, pay_t = pl.pallas_call(
        payload_kernel,
        out_shape=[shape(pay, BF16), shape(pay, BF16)],
        in_specs=[HBM] * 8,
        out_specs=[VMEM] * 2,
        scratch_shapes=[pltpu.VMEM((FEATS, PART), BF16)] * 2
        + [pltpu.VMEM((1, PART), F32)] * 6
        + [pltpu.VMEM((PART, LANES), F32), pltpu.SemaphoreType.DMA((8,))],
        compiler_params=params(24),
    )(
        *(
            pltpu.with_memory_space_constraint(value, pltpu.HBM)
            for value in (
                src_feat, tgt_feat, line(row_pot), line(col_pot), line(src_mass), line(tgt_mass),
                line(rhs_src), line(rhs_tgt),
            )
        )
    )
    s_parts, t_parts = gather_all(pay_s, pay_t)

    feats = shape((16, *pay), BF16)
    packed = shape((2 * 64, LANES))
    natural = shape((2 * BLOCKS, TILE))
    column = pltpu.VMEM((TILE, LANES), F32)
    kern, stored, xs, ys, pb, qb, rsum, csum = pl.pallas_call(
        build_kernel,
        out_shape=[
            pltpu.VMEM((SLOTS, TILE, TILE), F32), shape((SLOTS, TILE, TILE)),
            feats, feats, packed, natural, packed, packed,
        ],
        in_specs=[SMEM] + [ANY] * 7,
        out_specs=[VMEM, ANY] + [VMEM] * 6,
        scratch_shapes=[
            pltpu.VMEM((TILE, LANES), BF16),
            pltpu.VMEM((LANES, TILE), BF16),
            column,
            column,
            column,
            pltpu.VMEM((2 * BLOCKS, TILE), F32),
            pltpu.VMEM((4, 16, PART), F32),
            pltpu.SemaphoreType.DMA((32,)),
            pltpu.SemaphoreType.DMA((SLOTS,)),
        ],
        compiler_params=params(24),
    )(meta, *s_parts, *t_parts)
    kern = pltpu.with_memory_space_constraint(kern, pltpu.VMEM)

    rsum, csum = sum_pieces(rsum, csum)
    pv, qv, rimg, cimg = pl.pallas_call(
        apply_kernel,
        out_shape=[packed, natural, packed, packed],
        in_specs=[SMEM] + [VMEM] * 5,
        out_specs=[VMEM] * 4,
        scratch_shapes=[column, column, pltpu.VMEM((BLOCKS, TILE), F32)],
        compiler_params=params(24),
    )(meta, rsum, csum, pb, qb, kern)

    rimg, cimg = sum_pieces(rimg, cimg)
    pw, qw, dots, known = pl.pallas_call(
        form_kernel,
        out_shape=[shape((3 * 64, LANES)), shape((3 * BLOCKS, TILE))] + [shape((8, LANES))] * 2,
        in_specs=[SMEM] + [VMEM] * 7,
        out_specs=[VMEM] * 4,
        scratch_shapes=[column, pltpu.VMEM((8, LANES), F32)],
        compiler_params=params(24),
    )(meta, rimg, cimg, pb, qb, pv, qv, kern)

    dots = summed(summed(dots, "tgt"), "src")
    outs = pl.pallas_call(
        grad_kernel,
        out_shape=[shape((1, PART))] * 2
        + [shape((8, FEATS, PART))] * 2
        + [shape((4, FEATS, PART))] * 3
        + [shape((4, FEATS // 2, PART))] * 2,
        in_specs=[SMEM] + [VMEM] * 8 + [ANY],
        out_specs=[VMEM] * 9,
        scratch_shapes=[
            pltpu.VMEM((64, LANES), F32),
            pltpu.VMEM((BLOCKS, TILE), F32),
            column,
            pltpu.VMEM((TILE, TILE), BF16),
            pltpu.VMEM((BLOCKS, FEATS + 16, TILE), F32),
            pltpu.VMEM((BLOCKS, FEATS + 16, TILE), F32),
            pltpu.VMEM((3, TILE, TILE), F32),
            pltpu.SemaphoreType.DMA((3,)),
        ],
        compiler_params=params(40),
    )(meta, dots, known, pb, qb, pw, qw, xs, ys, stored)
    adj_s, adj_t = outs[:2]
    grad_src, grad_tgt = scatter_all(*outs[2:])
    return adj_s.reshape(PART), adj_t.reshape(PART), grad_src, grad_tgt


def solution(mesh):
    in_specs = (
        P(None, ("src", "tgt")),
        P(None, ("tgt", "src")),
        P(("src", "tgt")),
        P(("tgt", "src")),
        P(("src", "tgt")),
        P(("tgt", "src")),
        P(("src", "tgt")),
        P(("tgt", "src")),
        P("src", "tgt", None),
        P("src", "tgt", None),
        P("src", "tgt"),
    )
    out_specs = (
        P(("src", "tgt")),
        P(("tgt", "src")),
        P(None, ("src", "tgt")),
        P(None, ("tgt", "src")),
    )
    return jax.shard_map(shards, mesh=mesh, in_specs=in_specs, out_specs=out_specs, check_vma=False)
```

time: 272 us -> 250 us (0.919)
  waiting for transfers between devices: 95.6 us -> 65.8 us
  blocking collectives: 0 us -> 28.4 us
  starting transfers between devices: 131 us -> 105 us
  Pallas kernels: 20.9 us -> 30.6 us
  local copies, waits for them, and re-layouts: 9.77 us -> 6.04 us
    all_to_all x0 -> x2, blocking collectives: none -> 28.4 us  [exchange(): return lax.all_to_all(value, axis, 0, 0)]
    ppermute x26 -> x18, starting transfers between devices: 74.9 us -> 47.7 us  [swap(): return lax.ppermute(value, axis, [(i, i ^ mask) for i in range(16)])]
    ppermute x8, waiting for transfers between devices: 32.7 us -> 12.2 us  [along_x(): lax.ppermute(value, 'src', [(i, i // 4 * 4 + (i + step) % 4) for i in ran...]
    ppermute x26 -> x18, waiting for transfers between devices: 39.2 us -> 26.1 us  [swap(): return lax.ppermute(value, axis, [(i, i ^ mask) for i in range(16)])]
    ppermute x8, starting transfers between devices: 28.4 us -> 22.3 us  [along_x(): lax.ppermute(value, 'src', [(i, i // 4 * 4 + (i + step) % 4) for i in ran...]
    unnamed x67 -> x35, local copies, waits for them, and re-layouts: 9.12 us -> 3.98 us
    pallas_call x1, Pallas kernels: 7.78 us -> 12.5 us  [shards(): pl.pallas_call(build_kernel, out_shape=[pltpu.VMEM((SLOTS, TILE, TILE), F...]
    ppermute x14 -> x10, starting transfers between devices: 19.1 us -> 23.3 us  [along_z(): lax.ppermute(value, 'tgt', [(i, (i + 2 * step) % 16) for i in range(16)])]
  transfers between devices with their start and end apart: 55 -> 42, of which waited for: 35 -> 24; matrix products, arithmetic and copies ran while one was open for 2% -> 2% of each run, Pallas kernels for 0% -> 0%
where the time goes in v2:
time: 250 us; the launch traced here: 245 us
  starting transfers between devices  105 us (42%)
  waiting for transfers between devices  65.8 us (26%)
  Pallas kernels  30.6 us (12%)
  blocking collectives  28.4 us (11%)
  other arithmetic  7.47 us (3%)
  local copies, waits for them, and re-layouts  6.04 us (2%)
    ppermute x18, starting transfers between devices, swap(): return lax.ppermute(value, axis, [(i, i ^ mask) for i in range(16)])  47.7 us
    all_to_all x2, blocking collectives, exchange(): return lax.all_to_all(value, axis, 0, 0)  28.4 us
    ppermute x18, waiting for transfers between devices, swap(): return lax.ppermute(value, axis, [(i, i ^ mask) for i in range(16)])  26.1 us
    ppermute x10, waiting for transfers between devices, along_z(): lax.ppermute(value, 'tgt', [(i, (i + 2 * step) % 16) for i in range(16)])  25 us
    ppermute x10, starting transfers between devices, along_z(): lax.ppermute(value, 'tgt', [(i, (i + 2 * step) % 16) for i in range(16)])  23.3 us
    ppermute x8, starting transfers between devices, along_x(): lax.ppermute(value, 'src', [(i, i // 4 * 4 + (i + step) % 4) for i in ran...  22.3 us
    pallas_call x1, Pallas kernels, shards(): pl.pallas_call(build_kernel, out_shape=[pltpu.VMEM((SLOTS, TILE, TILE), F...  12.5 us
    ppermute x8, waiting for transfers between devices, along_x(): lax.ppermute(value, 'src', [(i, i // 4 * 4 + (i + step) % 4) for i in ran...  12.2 us
  transfers between devices with their start and end apart: 42, of which 24 were waited for; matrix products, arithmetic and copies ran while one was open for 2% of the time, Pallas kernels for 0%

profile of v2, /device:TPU:24, one launch (start us, length us, event | category | flops | bytes accessed | tf_op | source)
XLA Modules:
  0.0 244.7 jit_solution(18286461324559325862)
XLA Ops:
  6.5 7.2 %collective-permute-start.2 = (bf16[80,512]{1,0:T(8,128)(2,1)S(1)}, bf16[80,512]{1,0:T(8,128)(2,1)S(1)}, u32[]{:S(2)}, u32[]{:S(2)}) collective-permute-start(bf16[80,512]{1,0:T(8,128)(2,1)S(1)} %get-tuple-element.70), channel_id=1, source_target_pairs={{0,8},{1,9},{2,10},{3,11},{4,12},{5,13},{6,14},{7,15},{8,0},{9,1},... | collective-permute-start | bytes 245768 | tf_op jit(solution)/shard_map/ppermute | solution.py:526
  25.5 5.3 %collective-permute-done.9 = bf16[2,80,512]{2,1,0:T(8,128)(2,1)S(1)} collective-permute-done((bf16[2,80,512]{2,1,0:T(8,128)(2,1)S(1)}, bf16[2,80,512]{2,1,0:T(8,128)(2,1)S(1)}, u32[]{:S(2)}, u32[]{:S(2)}) %collective-permute-start.9) | collective-permute-done | bytes 163872 | tf_op jit(solution)/shard_map/ppermute | solution.py:526
  41.3 3.4 %collective-permute-done.11.t3 = bf16[2,80,512]{2,1,0:T(8,128)(2,1)S(1)} collective-permute-done((bf16[2,80,512]{2,1,0:T(8,128)(2,1)S(1)}, bf16[2,80,512]{2,1,0:T(8,128)(2,1)S(1)}, u32[]{:S(2)}, u32[]{:S(2)}) %collective-permute-start.11) | collective-permute-done | bytes 163872 | tf_op jit(solution)/shard_map/ppermute | solution.py:534
  46.2 12.5 %shard_map.139 = (f32[8,1024,1024]{2,1,0:T(8,128)S(1)}, f32[8,1024,1024]{2,1,0:T(8,128)}, bf16[16,80,512]{2,1,0:T(8,128)(2,1)}, bf16[16,80,512]{2,1,0:T(8,128)(2...) custom-call(s32[19]{0:T(128)} %concatenate.12.meta, ...), custom_call_target="tpu_custom_call" | custom-call | tf_op jit(solution)/shard_map/pallas_call | solution.py:643
  58.9 5.5 %collective-permute-start.14 = (f32[128,128]{1,0:T(8,128)}, f32[128,128]{1,0:T(8,128)S(1)}, u32[]{:S(2)}, u32[]{:S(2)}) collective-permute-start(f32[128,128]{1,0:T(8,128)} %get-tuple-element.83), channel_id=1, source_target_pairs={{0,16},{16,0},{32,48},{48,32},{64,80},{80,64},{96,112},{112,96},{1... | collective-permute-start | bytes 196616 | tf_op jit(solution)/shard_map/ppermute | solution.py:522
  67.9 14.2 %collective-permute-start.15 = (f32[128,128]{1,0:T(8,128)S(1)}, f32[128,128]{1,0:T(8,128)S(1)}, u32[]{:S(2)}, u32[]{:S(2)}) collective-permute-start(f32[128,128]{1,0:T(8,128)S(1)} %add.84), channel_id=1, source_target_pairs={{0,2},{1,3},{2,0},{3,1},{4,6},{5,7},{6,4},{7,5},{8,10},{9,11},{10,... | collective-permute-start | bytes 196616 | tf_op jit(solution)/shard_map/ppermute | solution.py:522
  84.4 3.5 %collective-permute-done.16 = f32[128,128]{1,0:T(8,128)S(1)} collective-permute-done((f32[128,128]{1,0:T(8,128)S(1)}, f32[128,128]{1,0:T(8,128)S(1)}, u32[]{:S(2)}, u32[]{:S(2)}) %collective-permute-start.16) | collective-permute-done | bytes 65568 | tf_op jit(solution)/shard_map/ppermute | solution.py:522
  89.3 4.1 %collective-permute-done.17 = f32[128,128]{1,0:T(8,128)S(1)} collective-permute-done((f32[128,128]{1,0:T(8,128)S(1)}, f32[128,128]{1,0:T(8,128)S(1)}, u32[]{:S(2)}, u32[]{:S(2)}) %collective-permute-start.17) | collective-permute-done | bytes 65568 | tf_op jit(solution)/shard_map/ppermute | solution.py:522
  93.4 4.3 %collective-permute-start.19 = (f32[128,128]{1,0:T(8,128)S(1)}, f32[128,128]{1,0:T(8,128)S(1)}, u32[]{:S(2)}, u32[]{:S(2)}) collective-permute-start(f32[128,128]{1,0:T(8,128)S(1)} %add.88), channel_id=1, source_target_pairs={{0,8},{1,9},{2,10},{3,11},{4,12},{5,13},{6,14},{7,15},{8,0},{9,1},... | collective-permute-start | bytes 196616 | tf_op jit(solution)/shard_map/ppermute | solution.py:522
  104.2 4.4 %shard_map.140 = (f32[128,128]{1,0:T(8,128)}, f32[16,1024]{1,0:T(8,128)}, f32[128,128]{1,0:T(8,128)}, f32[128,128]{1,0:T(8,128)}) custom-call(s32[19]{0:T(128)} %concatenate.12.meta, f32[128,128]{1,0:T(8,128)} %add.90.rows_in, f32[128,128]{1,0:T(8,128)} %add.91.cols_in, f32[128,128]{1,0:T(8,128)} %get-tuple-element.92.pb, f32[16,1024]{1,0:T(8,128)} %get-tuple-element.93.qb, ...), custom_call_target="tpu_custom_call" | custom-call | tf_op jit(solution)/shard_map/pallas_call | solution.py:667
  108.6 3.7 %collective-permute-start.22 = (f32[128,128]{1,0:T(8,128)}, f32[128,128]{1,0:T(8,128)S(1)}, u32[]{:S(2)}, u32[]{:S(2)}) collective-permute-start(f32[128,128]{1,0:T(8,128)} %get-tuple-element.96), channel_id=1, source_target_pairs={{0,16},{16,0},{32,48},{48,32},{64,80},{80,64},{96,112},{112,96},{1... | collective-permute-start | bytes 196616 | tf_op jit(solution)/shard_map/ppermute | solution.py:522
  116.0 5.0 %collective-permute-start.23 = (f32[128,128]{1,0:T(8,128)S(1)}, f32[128,128]{1,0:T(8,128)S(1)}, u32[]{:S(2)}, u32[]{:S(2)}) collective-permute-start(f32[128,128]{1,0:T(8,128)S(1)} %add.92), channel_id=1, source_target_pairs={{0,2},{1,3},{2,0},{3,1},{4,6},{5,7},{6,4},{7,5},{8,10},{9,11},{10,... | collective-permute-start | bytes 196616 | tf_op jit(solution)/shard_map/ppermute | solution.py:522
  123.3 3.5 %collective-permute-done.24 = f32[128,128]{1,0:T(8,128)S(1)} collective-permute-done((f32[128,128]{1,0:T(8,128)S(1)}, f32[128,128]{1,0:T(8,128)S(1)}, u32[]{:S(2)}, u32[]{:S(2)}) %collective-permute-start.24) | collective-permute-done | bytes 65568 | tf_op jit(solution)/shard_map/ppermute | solution.py:522
  135.5 3.9 %collective-permute-start.28 = (f32[128,128]{1,0:T(8,128)S(1)}, f32[128,128]{1,0:T(8,128)S(1)}, u32[]{:S(2)}, u32[]{:S(2)}) collective-permute-start(f32[128,128]{1,0:T(8,128)S(1)} %add.97), channel_id=1, source_target_pairs={{0,128},{16,144},{32,160},{48,176},{64,192},{80,208},{96,224},{112... | collective-permute-start | bytes 196616 | tf_op jit(solution)/shard_map/ppermute | solution.py:522
  142.6 3.4 %shard_map.141 = (f32[192,128]{1,0:T(8,128)}, f32[24,1024]{1,0:T(8,128)}, f32[8,128]{1,0:T(8,128)}, f32[8,128]{1,0:T(8,128)}) custom-call(s32[19]{0:T(128)} %concatenate.12.meta, f32[128,128]{1,0:T(8,128)} %add.98.rows_in, f32[128,128]{1,0:T(8,128)} %add.99.cols_in, f32[128,128]{1,0:T(8,128)} %get-tuple-element.92.pb, f32[16,1024]{1,0:T(8,128)} %get-tuple-element.93.qb, ...), custom_call_target="tpu_custom_call" | custom-call | tf_op jit(solution)/shard_map/pallas_call | solution.py:677
  146.7 14.8 %all_to_all.10 = f32[16,8,128]{2,1,0:T(8,128)S(1)} all-to-all(f32[16,8,128]{2,1,0:T(8,128)S(1)} %broadcast_in_dim.4), channel_id=1, replica_groups=mesh['src'=16,'tgt'=16] {'tgt'}, dimensions={0} | all-to-all | bytes 131072 | tf_op jit(solution)/shard_map/all_to_all | solution.py:538
  161.6 13.6 %all_to_all.11 = f32[16,8,128]{2,1,0:T(8,128)S(1)} all-to-all(f32[16,8,128]{2,1,0:T(8,128)S(1)} %broadcast_in_dim.5), channel_id=1, replica_groups=mesh['src'=16,'tgt'=16] {'src'}, dimensions={0} | all-to-all | bytes 131072 | tf_op jit(solution)/shard_map/all_to_all | solution.py:538
  177.7 8.1 %shard_map.142 = (f32[1,512]{1,0:T(1,128)}, f32[1,512]{1,0:T(1,128)}, f32[8,64,512]{2,1,0:T(8,128)S(1)}, f32[8,64,512]{2,1,0:T(8,128)S(1)}, f32[4,64,512]{2,1,0:...) custom-call(s32[19]{0:T(128)S(1)} %copy-done.6, ...), custom_call_target="tpu_custom_call" | custom-call | tf_op jit(solution)/shard_map/pallas_call | solution.py:687
  186.1 4.9 %collective-permute-start.30 = (f32[4,32,512]{2,1,0:T(8,128)S(1)}, f32[4,32,512]{2,1,0:T(8,128)S(1)}, u32[]{:S(2)}, u32[]{:S(2)}) collective-permute-start(f32[4,32,512]{2,1,0:T(8,128)S(1)} %get-tuple-element.118), channel_id=1, source_target_pairs={{0,16},{16,32},{32,48},{48,0},{64,80},{80,96},{96,112},{112,64},{1... | collective-permute-start | bytes 786440 | tf_op jit(solution)/shard_map/ppermute | solution.py:534
  191.0 8.2 %collective-permute-start.31 = (f32[4,32,512]{2,1,0:T(8,128)S(1)}, f32[4,32,512]{2,1,0:T(8,128)S(1)}, u32[]{:S(2)}, u32[]{:S(2)}) collective-permute-start(f32[4,32,512]{2,1,0:T(8,128)S(1)} %get-tuple-element.119), channel_id=1, source_target_pairs={{0,48},{16,0},{32,16},{48,32},{64,112},{80,64},{96,80},{112,96},{1... | collective-permute-start | bytes 786440 | tf_op jit(solution)/shard_map/ppermute | solution.py:534
  199.2 6.6 %collective-permute-done.30 = f32[4,32,512]{2,1,0:T(8,128)S(1)} collective-permute-done((f32[4,32,512]{2,1,0:T(8,128)S(1)}, f32[4,32,512]{2,1,0:T(8,128)S(1)}, u32[]{:S(2)}, u32[]{:S(2)}) %collective-permute-start.30) | collective-permute-done | bytes 262176 | tf_op jit(solution)/shard_map/ppermute | solution.py:534
  213.3 10.9 %collective-permute-done.35 = f32[2,64,512]{2,1,0:T(8,128)S(1)} collective-permute-done((f32[2,64,512]{2,1,0:T(8,128)S(1)}, f32[2,64,512]{2,1,0:T(8,128)S(1)}, u32[]{:S(2)}, u32[]{:S(2)}) %collective-permute-start.35) | collective-permute-done | bytes 262176 | tf_op jit(solution)/shard_map/ppermute | solution.py:526
  225.2 5.2 %collective-permute-start.38 = (f32[64,512]{1,0:T(8,128)S(1)}, f32[64,512]{1,0:T(8,128)S(1)}, u32[]{:S(2)}, u32[]{:S(2)}) collective-permute-start(f32[64,512]{1,0:T(8,128)S(1)} %get-tuple-element.136), channel_id=1, source_target_pairs={{0,8},{1,9},{2,10},{3,11},{4,12},{5,13},{6,14},{7,15},{8,0},{9,1},... | collective-permute-start | bytes 393224 | tf_op jit(solution)/shard_map/ppermute | solution.py:526
  237.1 3.5 %collective-permute-start.39 = (f32[64,512]{1,0:T(8,128)S(1)}, f32[64,512]{1,0:T(8,128)S(1)}, u32[]{:S(2)}, u32[]{:S(2)}) collective-permute-start(f32[64,512]{1,0:T(8,128)S(1)} %get-tuple-element.144), channel_id=1, source_target_pairs={{0,64},{16,80},{32,96},{48,112},{64,128},{80,144},{96,160},{112,17... | collective-permute-start | bytes 393224 | tf_op jit(solution)/shard_map/ppermute | solution.py:530
  (138 shorter events, 83.3 us)
Async XLA Ops:
  1.9 11.9 %collective-permute-start.5 = (bf16[80,512]{1,0:T(8,128)(2,1)S(1)}, bf16[80,512]{1,0:T(8,128)(2,1)S(1)}, u32[]{:S(2)}, u32[]{:S(2)}) collective-permute-start(bf16[80,512]{1,0:T(8,128)(2,1)S(1)} %get-tuple-element.71), channel_id=1, source_target_pairs={{0,128},{16,144},{32,160},{48,176},{64,192},{80,208},{96,224},{112... | collective-permute-start | bytes 245768 | tf_op jit(solution)/shard_map/ppermute | solution.py:530
  3.2 12.5 %collective-permute-start.4 = (bf16[80,512]{1,0:T(8,128)(2,1)S(1)}, bf16[80,512]{1,0:T(8,128)(2,1)S(1)}, u32[]{:S(2)}, u32[]{:S(2)}) collective-permute-start(bf16[80,512]{1,0:T(8,128)(2,1)S(1)} %get-tuple-element.71), channel_id=1, source_target_pairs={{0,192},{16,208},{32,224},{48,240},{64,0},{80,16},{96,32},{112,48}... | collective-permute-start | bytes 245768 | tf_op jit(solution)/shard_map/ppermute | solution.py:530
  4.8 10.9 %collective-permute-start.3 = (bf16[80,512]{1,0:T(8,128)(2,1)S(1)}, bf16[80,512]{1,0:T(8,128)(2,1)S(1)}, u32[]{:S(2)}, u32[]{:S(2)}) collective-permute-start(bf16[80,512]{1,0:T(8,128)(2,1)S(1)} %get-tuple-element.71), channel_id=1, source_target_pairs={{0,64},{16,80},{32,96},{48,112},{64,128},{80,144},{96,160},{112,17... | collective-permute-start | bytes 245768 | tf_op jit(solution)/shard_map/ppermute | solution.py:530
  6.5 10.3 %collective-permute-start.2 = (bf16[80,512]{1,0:T(8,128)(2,1)S(1)}, bf16[80,512]{1,0:T(8,128)(2,1)S(1)}, u32[]{:S(2)}, u32[]{:S(2)}) collective-permute-start(bf16[80,512]{1,0:T(8,128)(2,1)S(1)} %get-tuple-element.70), channel_id=1, source_target_pairs={{0,8},{1,9},{2,10},{3,11},{4,12},{5,13},{6,14},{7,15},{8,0},{9,1},... | collective-permute-start | bytes 245768 | tf_op jit(solution)/shard_map/ppermute | solution.py:526
  19.6 14.3 %collective-permute-start.7 = (bf16[4,80,512]{2,1,0:T(8,128)(2,1)S(1)}, bf16[4,80,512]{2,1,0:T(8,128)(2,1)S(1)}, u32[]{:S(2)}, u32[]{:S(2)}) collective-permute-start(bf16[4,80,512]{2,1,0:T(8,128)(2,1)S(1)} %pad_maximum_fusion.2.t0), channel_id=1, source_target_pairs={{0,48},{16,0},{32,16},{48,32},{64,112},{80,64},{96,80},{112,96},{1... | collective-permute-start | bytes 983048 | tf_op jit(solution)/shard_map/ppermute | solution.py:534
  22.4 11.4 %collective-permute-start.6 = (bf16[4,80,512]{2,1,0:T(8,128)(2,1)S(1)}, bf16[4,80,512]{2,1,0:T(8,128)(2,1)S(1)}, u32[]{:S(2)}, u32[]{:S(2)}) collective-permute-start(bf16[4,80,512]{2,1,0:T(8,128)(2,1)S(1)} %pad_maximum_fusion.2.t0), channel_id=1, source_target_pairs={{0,16},{16,32},{32,48},{48,0},{64,80},{80,96},{96,112},{112,64},{1... | collective-permute-start | bytes 983048 | tf_op jit(solution)/shard_map/ppermute | solution.py:534
  22.5 8.4 %collective-permute-start.9 = (bf16[2,80,512]{2,1,0:T(8,128)(2,1)S(1)}, bf16[2,80,512]{2,1,0:T(8,128)(2,1)S(1)}, u32[]{:S(2)}, u32[]{:S(2)}) collective-permute-start(bf16[2,80,512]{2,1,0:T(8,128)(2,1)S(1)} %get-tuple-element.151), channel_id=1, source_target_pairs={{0,12},{1,13},{2,14},{3,15},{4,0},{5,1},{6,2},{7,3},{8,4},{9,5},{1... | collective-permute-start | bytes 491528 | tf_op jit(solution)/shard_map/ppermute | solution.py:526
  25.2 8.6 %collective-permute-start.8 = (bf16[2,80,512]{2,1,0:T(8,128)(2,1)S(1)}, bf16[2,80,512]{2,1,0:T(8,128)(2,1)S(1)}, u32[]{:S(2)}, u32[]{:S(2)}) collective-permute-start(bf16[2,80,512]{2,1,0:T(8,128)(2,1)S(1)} %get-tuple-element.152), channel_id=1, source_target_pairs={{0,4},{1,5},{2,6},{3,7},{4,8},{5,9},{6,10},{7,11},{8,12},{9,13},{1... | collective-permute-start | bytes 491528 | tf_op jit(solution)/shard_map/ppermute | solution.py:526
  33.9 10.8 %collective-permute-start.10 = (bf16[8,80,512]{2,1,0:T(8,128)(2,1)S(1)}, bf16[8,80,512]{2,1,0:T(8,128)(2,1)S(1)}, u32[]{:S(2)}, u32[]{:S(2)}) collective-permute-start(bf16[8,80,512]{2,1,0:T(8,128)(2,1)S(1)} %constant_dynamic-update-slice_fusion.s0), channel_id=1, source_target_pairs={{0,1},{1,0},{2,3},{3,2},{4,5},{5,4},{6,7},{7,6},{8,9},{9,8},{10,11... | collective-permute-start | bytes 1966088 | tf_op jit(solution)/shard_map/ppermute | solution.py:522
  58.9 8.2 %collective-permute-start.14 = (f32[128,128]{1,0:T(8,128)}, f32[128,128]{1,0:T(8,128)S(1)}, u32[]{:S(2)}, u32[]{:S(2)}) collective-permute-start(f32[128,128]{1,0:T(8,128)} %get-tuple-element.83), channel_id=1, source_target_pairs={{0,16},{16,0},{32,48},{48,32},{64,80},{80,64},{96,112},{112,96},{1... | collective-permute-start | bytes 196616 | tf_op jit(solution)/shard_map/ppermute | solution.py:522
  67.9 16.5 %collective-permute-start.15 = (f32[128,128]{1,0:T(8,128)S(1)}, f32[128,128]{1,0:T(8,128)S(1)}, u32[]{:S(2)}, u32[]{:S(2)}) collective-permute-start(f32[128,128]{1,0:T(8,128)S(1)} %add.84), channel_id=1, source_target_pairs={{0,2},{1,3},{2,0},{3,1},{4,6},{5,7},{6,4},{7,5},{8,10},{9,11},{10,... | collective-permute-start | bytes 196616 | tf_op jit(solution)/shard_map/ppermute | solution.py:522
  93.4 8.4 %collective-permute-start.19 = (f32[128,128]{1,0:T(8,128)S(1)}, f32[128,128]{1,0:T(8,128)S(1)}, u32[]{:S(2)}, u32[]{:S(2)}) collective-permute-start(f32[128,128]{1,0:T(8,128)S(1)} %add.88), channel_id=1, source_target_pairs={{0,8},{1,9},{2,10},{3,11},{4,12},{5,13},{6,14},{7,15},{8,0},{9,1},... | collective-permute-start | bytes 196616 | tf_op jit(solution)/shard_map/ppermute | solution.py:522
  133.1 8.3 %collective-permute-start.27 = (f32[128,128]{1,0:T(8,128)S(1)}, f32[128,128]{1,0:T(8,128)S(1)}, u32[]{:S(2)}, u32[]{:S(2)}) collective-permute-start(f32[128,128]{1,0:T(8,128)S(1)} %add.96), channel_id=1, source_target_pairs={{0,8},{1,9},{2,10},{3,11},{4,12},{5,13},{6,14},{7,15},{8,0},{9,1},... | collective-permute-start | bytes 196616 | tf_op jit(solution)/shard_map/ppermute | solution.py:522
  185.8 20.0 %collective-permute-start.29 = (f32[8,64,512]{2,1,0:T(8,128)S(1)}, f32[8,64,512]{2,1,0:T(8,128)S(1)}, u32[]{:S(2)}, u32[]{:S(2)}) collective-permute-start(f32[8,64,512]{2,1,0:T(8,128)S(1)} %get-tuple-element.117), channel_id=1, source_target_pairs={{0,1},{1,0},{2,3},{3,2},{4,5},{5,4},{6,7},{7,6},{8,9},{9,8},{10,11... | collective-permute-start | bytes 3145736 | tf_op jit(solution)/shard_map/ppermute | solution.py:522
  186.1 19.6 %collective-permute-start.30 = (f32[4,32,512]{2,1,0:T(8,128)S(1)}, f32[4,32,512]{2,1,0:T(8,128)S(1)}, u32[]{:S(2)}, u32[]{:S(2)}) collective-permute-start(f32[4,32,512]{2,1,0:T(8,128)S(1)} %get-tuple-element.118), channel_id=1, source_target_pairs={{0,16},{16,32},{32,48},{48,0},{64,80},{80,96},{96,112},{112,64},{1... | collective-permute-start | bytes 786440 | tf_op jit(solution)/shard_map/ppermute | solution.py:534
  191.0 14.8 %collective-permute-start.31 = (f32[4,32,512]{2,1,0:T(8,128)S(1)}, f32[4,32,512]{2,1,0:T(8,128)S(1)}, u32[]{:S(2)}, u32[]{:S(2)}) collective-permute-start(f32[4,32,512]{2,1,0:T(8,128)S(1)} %get-tuple-element.119), channel_id=1, source_target_pairs={{0,48},{16,0},{32,16},{48,32},{64,112},{80,64},{96,80},{112,96},{1... | collective-permute-start | bytes 786440 | tf_op jit(solution)/shard_map/ppermute | solution.py:534
  206.0 19.1 %collective-permute-start.33 = (f32[4,64,512]{2,1,0:T(8,128)S(1)}, f32[4,64,512]{2,1,0:T(8,128)S(1)}, u32[]{:S(2)}, u32[]{:S(2)}) collective-permute-start(f32[4,64,512]{2,1,0:T(8,128)S(1)} %pad_maximum_fusion.1), channel_id=1, source_target_pairs={{0,48},{16,0},{32,16},{48,32},{64,112},{80,64},{96,80},{112,96},{1... | collective-permute-start | bytes 1572872 | tf_op jit(solution)/shard_map/ppermute | solution.py:534
  209.1 16.0 %collective-permute-start.32 = (f32[4,64,512]{2,1,0:T(8,128)S(1)}, f32[4,64,512]{2,1,0:T(8,128)S(1)}, u32[]{:S(2)}, u32[]{:S(2)}) collective-permute-start(f32[4,64,512]{2,1,0:T(8,128)S(1)} %pad_maximum_fusion), channel_id=1, source_target_pairs={{0,16},{16,32},{32,48},{48,0},{64,80},{80,96},{96,112},{112,64},{1... | collective-permute-start | bytes 1572872 | tf_op jit(solution)/shard_map/ppermute | solution.py:534
  209.5 14.7 %collective-permute-start.35 = (f32[2,64,512]{2,1,0:T(8,128)S(1)}, f32[2,64,512]{2,1,0:T(8,128)S(1)}, u32[]{:S(2)}, u32[]{:S(2)}) collective-permute-start(f32[2,64,512]{2,1,0:T(8,128)S(1)} %get-tuple-element.140), channel_id=1, source_target_pairs={{0,12},{1,13},{2,14},{3,15},{4,0},{5,1},{6,2},{7,3},{8,4},{9,5},{1... | collective-permute-start | bytes 786440 | tf_op jit(solution)/shard_map/ppermute | solution.py:526
  211.8 13.3 %collective-permute-start.34 = (f32[2,64,512]{2,1,0:T(8,128)S(1)}, f32[2,64,512]{2,1,0:T(8,128)S(1)}, u32[]{:S(2)}, u32[]{:S(2)}) collective-permute-start(f32[2,64,512]{2,1,0:T(8,128)S(1)} %get-tuple-element.141), channel_id=1, source_target_pairs={{0,4},{1,5},{2,6},{3,7},{4,8},{5,9},{6,10},{7,11},{8,12},{9,13},{1... | collective-permute-start | bytes 786440 | tf_op jit(solution)/shard_map/ppermute | solution.py:526
  225.2 11.9 %collective-permute-start.38 = (f32[64,512]{1,0:T(8,128)S(1)}, f32[64,512]{1,0:T(8,128)S(1)}, u32[]{:S(2)}, u32[]{:S(2)}) collective-permute-start(f32[64,512]{1,0:T(8,128)S(1)} %get-tuple-element.136), channel_id=1, source_target_pairs={{0,8},{1,9},{2,10},{3,11},{4,12},{5,13},{6,14},{7,15},{8,0},{9,1},... | collective-permute-start | bytes 393224 | tf_op jit(solution)/shard_map/ppermute | solution.py:526
  230.4 10.2 %collective-permute-start.37 = (f32[64,512]{1,0:T(8,128)S(1)}, f32[64,512]{1,0:T(8,128)S(1)}, u32[]{:S(2)}, u32[]{:S(2)}) collective-permute-start(f32[64,512]{1,0:T(8,128)S(1)} %get-tuple-element.137), channel_id=1, source_target_pairs={{0,14},{1,15},{2,0},{3,1},{4,2},{5,3},{6,4},{7,5},{8,6},{9,7},{10,... | collective-permute-start | bytes 393224 | tf_op jit(solution)/shard_map/ppermute | solution.py:526
  230.4 10.2 %collective-permute-start.36 = (f32[64,512]{1,0:T(8,128)S(1)}, f32[64,512]{1,0:T(8,128)S(1)}, u32[]{:S(2)}, u32[]{:S(2)}) collective-permute-start(f32[64,512]{1,0:T(8,128)S(1)} %get-tuple-element.138), channel_id=1, source_target_pairs={{0,2},{1,3},{2,4},{3,5},{4,6},{5,7},{6,8},{7,9},{8,10},{9,11},{10,... | collective-permute-start | bytes 393224 | tf_op jit(solution)/shard_map/ppermute | solution.py:526
  232.7 7.9 %collective-permute-start.41 = (f32[64,512]{1,0:T(8,128)S(1)}, f32[64,512]{1,0:T(8,128)S(1)}, u32[]{:S(2)}, u32[]{:S(2)}) collective-permute-start(f32[64,512]{1,0:T(8,128)S(1)} %get-tuple-element.142), channel_id=1, source_target_pairs={{0,128},{16,144},{32,160},{48,176},{64,192},{80,208},{96,224},{112... | collective-permute-start | bytes 393224 | tf_op jit(solution)/shard_map/ppermute | solution.py:530
  (33 other events, 526.5 us)
